TPU v7x, 512 devices: a whole 4x8x8 slice. The times are simulated.
512 devices in a mesh: ctx: 128 (over z, y, core), ch: 4 (over x).
Axes of the slice: x: 4, y: 8, z: 8, core: 2. Of those that a mesh axis runs over, the one named last changes fastest.
Arguments:
- streams: bfloat16 [3, 16384, 4096], P(None, 'ctx', 'ch'), may hold values from -6 to 6
- seq_lengths: int32 [8], replicated, may hold values from 1 to 8192, 16384 in all
- conv_weight: float32 [3, 7, 4096], P(None, None, 'ch'), may hold values from -2.4 to 2.4
- rate: float32 [4096, 16], P('ch'), may hold values from 2e-05 to 0.25
- modal_gain: float32 [4096, 16], P('ch'), may hold values from -1.8 to 1.8
- cotangent: bfloat16 [16384, 4096], P('ctx', 'ch'), may hold values from -6 to 6
Outputs:
- output: bfloat16 [16384, 4096], P('ctx', 'ch')
- stream_grads: bfloat16 [3, 16384, 4096], P(None, 'ctx', 'ch')
- clipped_weight_grad: float32 [3, 7, 4096], P(None, None, 'ch')
Inputs may be any that keep to these rules, and one draw needn't show every extreme that they name: `seq_lengths`: 8 sequences that fill the 16384 positions in order; the longest is exactly 8192.
All inputs are finite; a program needn't handle non-finite values.
Results may differ from a plain program's by a relative error of at most 0.0057.
Values may be sent and summed in bfloat16 or wider, within the bound.
No kernel may reach another device: no remote copies, remote signals or barrier semaphores. Data moves between devices by JAX's collectives and lax.ppermute only.
A program may use at most 128 MiB of HBM per device.

v0:
```python
import functools

import jax
import jax.numpy as jnp
from jax import lax
from jax.experimental import pallas as pl
from jax.experimental.pallas import tpu as pltpu
from jax.sharding import PartitionSpec as P

F32 = jnp.float32
BF16 = jnp.bfloat16
TAPS = 7
REACH = TAPS - 1
TOK = 128
LANES = 128
OWN = 8
SUB = 8

LEFT = LANES - 3 * REACH
RIGHT = 0
STATE = 18
MODES = 16
GRADS = STATE + 4 * MODES


def rounded(value):
    return value.astype(BF16).astype(F32)


def halves(value):
    high = value.astype(BF16)
    return high, (value - high.astype(F32)).astype(BF16)


def one_minus_exp(x):
    series = jnp.full_like(x, 1.0)
    for n in range(11, 1, -1):
        series = 1.0 - (x * F32(1.0 / n)) * series
    return x * series


def gains(rate, gain):
    return gain * jnp.sqrt(one_minus_exp(2.0 * rate))


def start_list(seq_ref):
    starts = [jnp.int32(0)]
    for n in range(seq_ref.shape[0]):
        starts.append(starts[-1] + seq_ref[n])
    return starts


def dot(a, b):
    return lax.dot_general(a, b, (((1,), (0,)), ((), ())), preferred_element_type=F32)


def dot_t(a, b):
    return lax.dot_general(a, b, (((1,), (1,)), ((), ())), preferred_element_type=F32)


def turn_kernel(streams, cotangent, out):
    for pair in range(2):
        for k in range(SUB):
            cols = pl.ds(k * LANES, LANES)
            first = streams[2 * pair, :, cols]
            second = streams[1, :, cols] if pair == 0 else cotangent[:, cols]
            a = first.astype(F32).T.reshape(LANES // OWN, OWN, TOK)
            b = second.astype(F32).T.reshape(LANES // OWN, OWN, TOK)
            out[pl.ds(k * (LANES // OWN), LANES // OWN), pl.ds(pair * 16, 16), :] = (
                jnp.concatenate([a, b], axis=1).astype(BF16)
            )


ROWS_OF = (0, 8, 16, 24)


def owner_kernel(
    total, seq, moved, weight, rate, gain, out, sh, wide, u, dz, kc, vc, zs, ds, pay, fixf, fixb, prm
):
    blocks = moved.shape[0]
    index = lax.axis_index("ctx")
    starts = start_list(seq)
    starts[-1] = jnp.int32(total)
    nseq = seq.shape[0]
    lane = lax.broadcasted_iota(jnp.int32, (SUB, LANES), 1)

    chunk = pl.multiple_of((index // (LANES // OWN)) * LANES, LANES)
    back = lax.rem(LANES - lax.rem(index, LANES // OWN) * OWN, LANES)
    cols = pl.ds(chunk, LANES)
    prm[...] = jnp.zeros_like(prm)
    prm[0:MODES, :] = pltpu.roll(rate[:, cols], back, 1)
    prm[MODES : 2 * MODES, :] = pltpu.roll(gain[:, cols], back, 1)
    for i in range(3):
        prm[32 + 8 * i : 32 + 8 * i + TAPS, :] = weight[i, :, cols]
    prm[32:56, :] = pltpu.roll(prm[32:56, :], back, 1)
    own = prm[...].T[0:OWN, :]
    for i in range(3):
        for j in range(TAPS):
            f = 32 + 8 * i + j
            wide[i * TAPS + j] = jnp.broadcast_to(own[:, f : f + 1], (SUB, LANES))
    rate_rows = jnp.concatenate(
        [jnp.broadcast_to(own[:, m : m + 1], (SUB, LANES)) for m in range(MODES)], axis=0
    )
    gain_rows = jnp.concatenate(
        [
            jnp.broadcast_to(own[:, MODES + m : MODES + m + 1], (SUB, LANES))
            for m in range(MODES)
        ],
        axis=0,
    )
    coef_rows = gains(rate_rows, gain_rows)

    def filtering(b, masked):
        now = moved[b].astype(F32)
        before = moved[jnp.maximum(b - 1, 0)].astype(F32)
        if masked:
            place = b * TOK + lane
            since = jnp.zeros((SUB, LANES), jnp.int32)
            for s in starts[:-1]:
                since = jnp.where(s <= place, s, since)
            since = place - since
        done = []
        for i in range(3):
            x = now[ROWS_OF[i] : ROWS_OF[i] + 8]
            p = before[ROWS_OF[i] : ROWS_OF[i] + 8]
            acc = wide[i * TAPS] * x
            for j in range(1, TAPS):
                moved_x = pltpu.roll(jnp.where(lane >= LANES - j, p, x), j, 1)
                if masked:
                    moved_x = jnp.where(since >= j, moved_x, 0.0)
                sh[i * REACH + j - 1, b] = moved_x
                acc = acc + wide[i * TAPS + j] * moved_x
            done.append(acc)
        rows = pl.ds(pl.multiple_of(b * SUB, SUB), SUB)
        u[rows, :] = rounded(done[1] * done[2])
        dz[rows, :] = rounded(now[24:32] * done[0])
        kc[rows, :] = done[1]
        vc[rows, :] = done[2]

    def filter_loop(b, _):
        filtering(b, False)
        return 0

    lax.fori_loop(0, blocks, filter_loop, 0, unroll=2)
    for s in starts[:-1]:
        b = s // TOK
        filtering(b, True)
        filtering(jnp.minimum(b + 1, blocks - 1), True)

    for n in range(nseq):
        b = starts[n] // TOK
        rows = pl.ds(pl.multiple_of(b * SUB, SUB), SUB)
        place = b * TOK + lane
        fixf[n * SUB : (n + 1) * SUB, :] = jnp.where(place >= starts[n], u[rows, :], 0.0)
        fixb[n * SUB : (n + 1) * SUB, :] = jnp.where(place < starts[n], dz[rows, :], 0.0)

    row = lax.broadcasted_iota(jnp.int32, (blocks, TOK), 0)
    col = lax.broadcasted_iota(jnp.int32, (blocks, TOK), 1)
    head = jnp.ones((blocks, TOK), F32)
    tail = jnp.ones((blocks, TOK), F32)
    for s in starts[:-1]:
        here = row == s // TOK
        head = jnp.where(here & (col >= lax.rem(s, TOK)), 0.0, head)
        tail = jnp.where(here & (col < lax.rem(s, TOK)), 0.0, tail)

    lag = lax.broadcasted_iota(jnp.int32, (LANES, LANES), 1).astype(F32)
    ending = halves(jnp.exp(-rate_rows * (TOK - 1.0 - lag)))
    opening = halves(jnp.exp(-rate_rows * lag))
    lead_f = halves(coef_rows * jnp.exp(-rate_rows * (lag + 1.0)))
    lead_b = halves(coef_rows * jnp.exp(-rate_rows * (TOK - lag)))
    whole = jnp.exp(-rate_rows * TOK).T[0:1, :]
    taps = (coef_rows * jnp.exp(-rate_rows * lag)).reshape(MODES, OWN, LANES).sum(axis=0)

    mine = lax.rem(lax.broadcasted_iota(jnp.int32, (blocks, LANES), 1), OWN)
    end_f = jnp.zeros((blocks, LANES), F32)
    end_b = jnp.zeros((blocks, LANES), F32)
    for c in range(OWN):
        uc = (u[pl.ds(c, blocks, stride=OWN), :] * tail).astype(BF16)
        dc = (dz[pl.ds(c, blocks, stride=OWN), :] * head).astype(BF16)
        ef = dot_t(uc, ending[0]) + dot_t(uc, ending[1])
        eb = dot_t(dc, opening[0]) + dot_t(dc, opening[1])
        end_f = jnp.where(mine == c, ef, end_f)
        end_b = jnp.where(mine == c, eb, end_b)

    keep_f = head[:, TOK - 1 : TOK] * whole
    keep_b = keep_f
    step = 1
    while step < blocks:
        low = row >= step
        end_f = end_f + jnp.where(low, keep_f * pltpu.roll(end_f, step, 0), 0.0)
        keep_f = jnp.where(low, keep_f * pltpu.roll(keep_f, step, 0), 0.0)
        high = row < blocks - step
        end_b = end_b + jnp.where(high, keep_b * pltpu.roll(end_b, blocks - step, 0), 0.0)
        keep_b = jnp.where(high, keep_b * pltpu.roll(keep_b, blocks - step, 0), 0.0)
        step *= 2
    state_f = jnp.where(row >= 1, pltpu.roll(end_f, 1, 0), 0.0)
    state_b = jnp.where(row < blocks - 1, pltpu.roll(end_b, blocks - 1, 0), 0.0)
    sf = halves(state_f)
    sb = halves(state_b)

    pick_row = lax.broadcasted_iota(jnp.int32, (LANES, LANES), 0)
    pick_col = lax.broadcasted_iota(jnp.int32, (LANES, LANES), 1)
    zero = jnp.zeros((blocks, LANES), BF16)
    for c in range(OWN):
        strip = jnp.broadcast_to(taps[c : c + 1, :], (LANES, LANES))
        strip = pltpu.roll(strip, 0, 1, stride=1, stride_axis=0)
        kern = halves(jnp.where(pick_col >= pick_row, strip, 0.0))
        of_c = mine == c
        uc = jnp.concatenate(
            [u[pl.ds(c, blocks, stride=OWN), :], fixf[pl.ds(c, nseq, stride=OWN), :]], axis=0
        ).astype(BF16)
        dc = jnp.concatenate(
            [dz[pl.ds(c, blocks, stride=OWN), :], fixb[pl.ds(c, nseq, stride=OWN), :]], axis=0
        ).astype(BF16)
        zc = dot(uc, kern[0]) + dot(uc, kern[1])
        rc = dot_t(dc, kern[0]) + dot_t(dc, kern[1])
        fixf[pl.ds(c, nseq, stride=OWN), :] = zc[blocks:]
        fixb[pl.ds(c, nseq, stride=OWN), :] = rc[blocks:]
        fh, fl = [jnp.where(of_c, x, zero) for x in sf]
        bh, bl = [jnp.where(of_c, x, zero) for x in sb]
        carry_f = dot(fh, lead_f[0]) + dot(fh, lead_f[1]) + dot(fl, lead_f[0])
        carry_b = dot(bh, lead_b[0]) + dot(bh, lead_b[1]) + dot(bl, lead_b[0])
        zs[pl.ds(c, blocks, stride=OWN), :] = zc[:blocks] + head * carry_f
        ds[pl.ds(c, blocks, stride=OWN), :] = rc[:blocks] + tail * carry_b
        spread = jnp.zeros((blocks, LANES), F32)
        for g, part in enumerate((fh, fl, bh, bl)):
            goes = (lax.rem(pick_row, OWN) == c) & (
                pick_col == STATE + g * MODES + pick_row // OWN
            )
            spread = spread + dot(part, jnp.where(goes, 1.0, 0.0).astype(BF16))
        pay[pl.ds(c, blocks, stride=OWN), :] = spread
    for n in range(nseq):
        b = starts[n] // TOK
        rows = pl.ds(pl.multiple_of(b * SUB, SUB), SUB)
        place = b * TOK + lane
        fresh = (place >= starts[n]) & (place < starts[n + 1])
        zs[rows, :] = jnp.where(fresh, fixf[n * SUB : (n + 1) * SUB, :], zs[rows, :])
        if n > 0:
            fresh = (place >= starts[n - 1]) & (place < starts[n])
            ds[rows, :] = jnp.where(fresh, fixb[n * SUB : (n + 1) * SUB, :], ds[rows, :])

    def gradient(b, acc):
        rows = pl.ds(pl.multiple_of(b * SUB, SUB), SUB)
        now = moved[b].astype(F32)
        z = rounded(zs[rows, :])
        d = rounded(ds[rows, :])
        df = (now[24:32] * z, d * vc[rows, :], d * kc[rows, :])
        new = []
        for i in range(3):
            new.append(acc[i * TAPS] + df[i] * now[ROWS_OF[i] : ROWS_OF[i] + 8])
            for j in range(1, TAPS):
                new.append(acc[i * TAPS + j] + df[i] * sh[i * REACH + j - 1, b])
        halo = jnp.where(lane < REACH, df[0], 0.0)
        for i in (1, 2):
            part = pltpu.roll(df[i], i * REACH, 1)
            halo = jnp.where((lane >= i * REACH) & (lane < (i + 1) * REACH), part, halo)
        target = pl.ds(pl.multiple_of(jnp.maximum(b - 1, 0) * SUB, SUB), SUB)
        pay[target, :] = pay[target, :] + jnp.where(b > 0, halo, 0.0)
        return tuple(new)

    acc = lax.fori_loop(
        0, blocks, gradient, tuple(jnp.zeros((SUB, LANES), F32) for _ in range(3 * TAPS))
    )
    grads = jnp.zeros((SUB, LANES), F32)
    for f in range(3 * TAPS):
        grads = jnp.where(lane == GRADS + f, jnp.sum(acc[f], axis=1, keepdims=True), grads)

    def finish(p, _):
        tiles = []
        for b in (2 * p, 2 * p + 1):
            before = moved[jnp.maximum(b - 1, 0)].astype(F32)
            value = pay[pl.ds(pl.multiple_of(b * SUB, SUB), SUB), :] + grads
            for i in range(3):
                x = before[ROWS_OF[i] : ROWS_OF[i] + 8]
                first = LEFT + i * REACH
                x = x if i == 2 else pltpu.roll(x, first - (TOK - REACH) + LANES, 1)
                value = jnp.where((lane >= first) & (lane < first + REACH), x, value)
            tiles.append(value)
        out[pl.ds(pl.multiple_of(p * 16, 16), 16), :] = jnp.concatenate(tiles, axis=0).astype(BF16)
        return 0

    lax.fori_loop(0, blocks // 2, finish, 0)


def shard_kernel(
    total,
    seq,
    streams,
    cotangent,
    fields,
    weight,
    rate,
    gain,
    out,
    grads_out,
    wgrad,
    squares,
    xs,
    cots,
    fs,
    ws,
    prm,
    kcs,
    vcs,
    dzs,
    dfs,
    outs,
    sgs,
):
    index = lax.axis_index("ctx")
    local = [s - index * TOK for s in start_list(seq)]
    local[-1] = total - index * TOK

    for k in range(SUB):
        cols = pl.ds(k * LANES, LANES)
        turned = fields[pl.ds(k * LANES, LANES), :].astype(F32).T
        for g in range(LANES // 8):
            fs[pl.ds(g * 64 + k, 8, stride=SUB), :] = turned[g * 8 : g * 8 + 8]
        for g in range(MODES // 8):
            r = rate[g * 8 : g * 8 + 8, cols]
            prm[pl.ds(g * 64 + k, 8, stride=SUB), :] = jnp.exp(-r)
            prm[pl.ds(MODES * SUB + g * 64 + k, 8, stride=SUB), :] = gains(
                r, gain[g * 8 : g * 8 + 8, cols]
            )
        for i in range(3):
            ws[pl.ds(i * 64 + k, TAPS, stride=SUB), :] = weight[i, :, cols]
        for g in range(TOK // 16):
            for i in range(4):
                x = streams[i, pl.ds(g * 16, 16), cols] if i < 3 else cotangent[pl.ds(g * 16, 16), cols]
                x = x.astype(F32)
                for h in range(2):
                    t = g * 16 + h * 8
                    if i < 3:
                        xs[i, pl.ds((t + REACH) * SUB + k, 8, stride=SUB), :] = x[h * 8 : h * 8 + 8]
                    else:
                        cots[pl.ds(t * SUB + k, 8, stride=SUB), :] = x[h * 8 : h * 8 + 8]
    for i in range(3):
        xs[i, 0 : REACH * SUB, :] = fs[(LEFT + i * REACH) * SUB : (LEFT + (i + 1) * REACH) * SUB, :]
        dfs[i, TOK * SUB : (TOK + REACH) * SUB, :] = fs[
            (RIGHT + i * REACH) * SUB : (RIGHT + (i + 1) * REACH) * SUB, :
        ]

    def tile(ref, n):
        return ref[pl.ds(n * SUB, SUB), :]

    def at(ref, t):
        return ref[pl.ds(pl.multiple_of(t * SUB, SUB), SUB), :]

    def at3(ref, i, t):
        return ref[i, pl.ds(pl.multiple_of(t * SUB, SUB), SUB), :]

    def put(ref, t, value):
        ref[pl.ds(pl.multiple_of(t * SUB, SUB), SUB), :] = value

    def put3(ref, i, t, value):
        ref[i, pl.ds(pl.multiple_of(t * SUB, SUB), SUB), :] = value

    def since(t):
        last = local[0]
        for s in local[1:]:
            last = jnp.where(s <= t, s, last)
        return t - last

    def until(t):
        following = local[-1]
        for s in local[-2::-1]:
            following = jnp.where(s > t, s, following)
        return following - t

    def near(t0):
        found = jnp.bool_(False)
        for s in local:
            found = found | ((s >= t0 - REACH) & (s < t0 + 8 + REACH + 1))
        return found

    def forward(t0, state, masked):
        ages = [since(t0 + r) for r in range(8)] if masked else None
        done = []
        for i in range(3):
            w = [tile(ws, i * 8 + j) for j in range(TAPS)]
            x = [at3(xs, i, t0 + n) for n in range(8 + REACH)]
            row = []
            for r in range(8):
                acc = w[0] * x[r + REACH]
                for j in range(1, TAPS):
                    term = w[j] * x[r + REACH - j]
                    if masked:
                        term = jnp.where(ages[r] >= j, term, 0.0)
                    acc = acc + term
                row.append(acc)
            done.append(row)
        state = list(state)
        for r in range(8):
            t = t0 + r
            q, k, v = done[0][r], done[1][r], done[2][r]
            put(kcs, t, k)
            put(vcs, t, v)
            c = at(cots, t)
            put(dzs, t, rounded(c * q))
            u = rounded(k * v)
            z = jnp.zeros((SUB, LANES), F32)
            for m in range(MODES):
                old = state[m]
                if masked:
                    old = jnp.where(ages[r] > 0, old, 0.0)
                state[m] = tile(prm, m) * old + u
                z = z + tile(prm, MODES + m) * state[m]
            z = rounded(z)
            put(outs, t, q * z)
            put3(dfs, 0, t, c * z)
        return tuple(state)

    def backward(t0, state, masked):
        gaps = [until(t0 + r) for r in range(8)] if masked else None
        state = list(state)
        for r in range(7, -1, -1):
            t = t0 + r
            g = at(dzs, t)
            d = jnp.zeros((SUB, LANES), F32)
            for m in range(MODES):
                old = state[m]
                if masked:
                    old = jnp.where(gaps[r] > 1, old, 0.0)
                state[m] = tile(prm, m) * old + g
                d = d + tile(prm, MODES + m) * state[m]
            d = rounded(d)
            put3(dfs, 1, t, d * at(vcs, t))
            put3(dfs, 2, t, d * at(kcs, t))
        for i in range(3):
            w = [tile(ws, i * 8 + j) for j in range(TAPS)]
            y = [at3(dfs, i, t0 + n) for n in range(8 + REACH)]
            for r in range(8):
                acc = w[0] * y[r]
                for j in range(1, TAPS):
                    term = w[j] * y[r + j]
                    if masked:
                        term = jnp.where(gaps[r] > j, term, 0.0)
                    acc = acc + term
                put3(sgs, i, t0 + r, acc)
        return tuple(state)

    def entering(g):
        return tuple(
            tile(fs, STATE + g * MODES + m) + tile(fs, STATE + (g + 1) * MODES + m)
            for m in range(MODES)
        )

    def step_f(n, state):
        t0 = n * 8
        return lax.cond(
            near(t0),
            lambda s: forward(t0, s, True),
            lambda s: forward(t0, s, False),
            state,
        )

    def step_b(n, state):
        t0 = TOK - 8 - n * 8
        return lax.cond(
            near(t0),
            lambda s: backward(t0, s, True),
            lambda s: backward(t0, s, False),
            state,
        )

    lax.fori_loop(0, TOK // 8, step_f, entering(0))
    lax.fori_loop(0, TOK // 8, step_b, entering(2))

    total_sq = jnp.zeros((SUB, LANES), F32)
    for f in range(3 * TAPS):
        g = tile(fs, GRADS + f)
        total_sq = total_sq + g * g
    squares[...] = jnp.broadcast_to(jnp.sum(total_sq), (1, LANES))
    for k in range(SUB):
        cols = pl.ds(k * LANES, LANES)
        for i in range(3):
            wgrad[i, :, cols] = fs[pl.ds((GRADS + i * TAPS) * SUB + k, TAPS, stride=SUB), :]
        for g in range(TOK // 16):
            for i in range(4):
                parts = []
                for h in range(2):
                    rows = pl.ds((g * 16 + h * 8) * SUB + k, 8, stride=SUB)
                    parts.append(sgs[i, rows, :] if i < 3 else outs[rows, :])
                both = jnp.concatenate(parts, axis=0).astype(BF16)
                if i < 3:
                    grads_out[i, pl.ds(g * 16, 16), cols] = both
                else:
                    out[pl.ds(g * 16, 16), cols] = both


def vmem():
    return pl.BlockSpec(memory_space=pltpu.VMEM)


def smem():
    return pl.BlockSpec(memory_space=pltpu.SMEM)


def body(streams, seq_lengths, conv_weight, rate, modal_gain, cotangent):
    tok, chans = streams.shape[1:]
    shards = lax.axis_size("ctx")
    total = tok * shards
    rate_t, gain_t = rate.T, modal_gain.T
    params = pltpu.CompilerParams(vmem_limit_bytes=48 * 1024 * 1024)
    turned = pl.pallas_call(
        turn_kernel,
        out_shape=jax.ShapeDtypeStruct((shards, 4 * OWN, tok), BF16),
        in_specs=[vmem()] * 2,
        out_specs=vmem(),
        compiler_params=params,
        name="turn",
    )(streams, cotangent)
    moved = lax.all_to_all(turned, "ctx", split_axis=0, concat_axis=0, tiled=True)
    rows = shards * OWN
    plane = pltpu.VMEM((rows, LANES), F32)
    payload = pl.pallas_call(
        functools.partial(owner_kernel, total),
        out_shape=jax.ShapeDtypeStruct((rows, LANES), BF16),
        in_specs=[smem()] + [vmem()] * 4,
        out_specs=vmem(),
        scratch_shapes=[
            pltpu.VMEM((3 * REACH, shards, SUB, LANES), F32),
            pltpu.VMEM((3 * TAPS, SUB, LANES), F32),
        ]
        + [plane] * 7
        + [pltpu.VMEM((8 * SUB, LANES), F32)] * 2
        + [pltpu.VMEM((LANES, LANES), F32)],
        compiler_params=params,
        name="owner",
    )(seq_lengths, moved, conv_weight, rate_t, gain_t)
    fields = lax.all_to_all(
        payload.reshape(shards, OWN, LANES), "ctx", split_axis=0, concat_axis=0, tiled=True
    ).reshape(rows, LANES)
    plane = pltpu.VMEM((tok * SUB, LANES), F32)
    tall = pltpu.VMEM((3, (tok + REACH) * SUB, LANES), F32)
    output, stream_grads, weight_grad, squares = pl.pallas_call(
        functools.partial(shard_kernel, total),
        out_shape=[
            jax.ShapeDtypeStruct((tok, chans), BF16),
            jax.ShapeDtypeStruct((3, tok, chans), BF16),
            jax.ShapeDtypeStruct((3, TAPS, chans), F32),
            jax.ShapeDtypeStruct((1, LANES), F32),
        ],
        in_specs=[smem()] + [vmem()] * 6,
        out_specs=[vmem()] * 4,
        scratch_shapes=[
            tall,
            plane,
            pltpu.VMEM((LANES * SUB, LANES), F32),
            pltpu.VMEM((3 * 8 * SUB, LANES), F32),
            pltpu.VMEM((2 * MODES * SUB, LANES), F32),
            plane,
            plane,
            plane,
            tall,
            plane,
            pltpu.VMEM((3, tok * SUB, LANES), F32),
        ],
        compiler_params=params,
        name="shard",
    )(seq_lengths, streams, cotangent, fields, conv_weight, rate_t, gain_t)
    squares = lax.psum(squares[0, 0], "ch")
    factor = jnp.minimum(jnp.float32(1.0), 1.0 / jnp.sqrt(squares + 1e-06))
    return output, stream_grads, weight_grad * factor


def solution(mesh):
    return jax.shard_map(
        body,
        mesh=mesh,
        in_specs=(
            P(None, "ctx", "ch"),
            P(),
            P(None, None, "ch"),
            P("ch", None),
            P("ch", None),
            P("ctx", "ch"),
        ),
        out_specs=(P("ctx", "ch"), P(None, "ctx", "ch"), P(None, None, "ch")),
        check_vma=False,
    )
```

profile of v0, /device:TPU:1, one launch (start us, length us, event | category | flops | bytes accessed | tf_op | source)
XLA Modules:
  0.0 118.0 jit_solution(8476461338881804638)
XLA Ops:
  0.6 0.0 copy-start
  0.6 1.1 copy-done
  1.8 0.0 copy-start.2
  1.8 0.9 copy-done.2
  2.7 0.3 turn.1
  3.1 0.0 copy-start.4
  3.1 0.0 copy-start.5
  3.1 0.0 copy-start.6
  3.1 49.3 %all_to_all.10.moved = bf16[128,32,128]{2,1,0:T(8,128)(2,1)S(1)} all-to-all(bf16[128,32,128]{2,1,0:T(8,128)(2,1)S(1)} %turn.1), channel_id=1, replica_groups=mesh['ctx'=128,'ch'=4] {'ctx'}, dimensions={0} | all-to-all | bytes 2097152 | tf_op jit(solution)/shard_map/all_to_all | solution.py:513
  52.4 0.0 copy-start.7
  52.4 0.0 copy-done.4
  52.4 0.0 copy-done.5
  52.4 0.0 copy-done.6
  52.4 0.6 copy-done.7
  53.0 0.0 copy-start.1
  53.0 25.2 %owner.1 = bf16[1024,128]{1,0:T(8,128)(2,1)S(1)} custom-call(s32[8]{0:T(128)S(1)} %copy-done.7, bf16[128,32,128]{2,1,0:T(8,128)(2,1)S(1)} %all_to_all.10.moved, f32[3,7,1024]{2,1,0:T(8,128)S(1)} %copy-done.4, f32[16,1024]{1,0:T(8,128)S(1)} %bitcast.8, f32[16,1024]{1,0:T(8,128)S(1)} %bitcast.10), custom_call_target="tpu_custom_call" | custom-call | tf_op jit(solution)/shard_map/owner/pallas_call | solution.py:516
  78.2 0.0 copy-start.3
  78.2 21.7 %all_to_all.11 = bf16[128,8,128]{2,1,0:T(8,128)(2,1)S(1)} all-to-all(bf16[128,8,128]{2,1,0:T(8,128)(2,1)S(1)} %bitcast.7), channel_id=1, replica_groups=mesh['ctx'=128,'ch'=4] {'ctx'}, dimensions={0} | all-to-all | bytes 524288 | tf_op jit(solution)/shard_map/all_to_all | solution.py:531
  99.9 0.0 copy-done.1
  99.9 0.0 copy-done.3
  99.9 7.8 %shard.1 = (bf16[128,1024]{1,0:T(8,128)(2,1)}, bf16[3,128,1024]{2,1,0:T(8,128)(2,1)}, f32[3,7,1024]{2,1,0:T(8,128)S(1)}, f32[1,128]{1,0:T(1,128)S(1)}) custom-call(s32[8]{0:T(128)S(1)} %copy-done.7, bf16[3,128,1024]{2,1,0:T(8,128)(2,1)S(1)} %copy-done.1, bf16[128,1024]{1,0:T(8,128)(2,1)S(1)} %copy-done.3, bf16[1024,128]{1,0:T(8,128)(2,1)S(1)} %bitcast.6, ...), custom_call_target="tpu_custom_call" | custom-call | tf_op jit(solution)/shard_map/shard/pallas_call | solution.py:536
  107.7 9.0 %psum.7 = f32[]{:T(128)} all-reduce(f32[]{:T(128)S(1)} %bitcast.12), channel_id=1, replica_groups=mesh['ctx'=128,'ch'=4] {'ch'}, use_global_device_ids=true, to_apply=%region_0.0 | all-reduce | flops 1 | bytes 8 | tf_op jit(solution)/shard_map/psum | solution.py:562
  117.4 0.6 broadcast_multiply_fusion
Async XLA Ops:
  0.6 1.1 copy-start
  1.8 0.9 copy-start.2
  3.1 49.3 %copy-start.4 = (f32[3,7,1024]{2,1,0:T(8,128)S(1)}, f32[3,7,1024]{2,1,0:T(8,128)}, u32[]{:S(2)}) copy-start(f32[3,7,1024]{2,1,0:T(8,128)} %weight.3) | copy-start | bytes 258052
  3.1 49.3 %copy-start.5 = (f32[1024,16]{0,1:T(8,128)S(1)}, f32[1024,16]{0,1:T(8,128)}, u32[]{:S(2)}) copy-start(f32[1024,16]{0,1:T(8,128)} %param.9) | copy-start | bytes 196612
  3.1 49.3 %copy-start.6 = (f32[1024,16]{0,1:T(8,128)S(1)}, f32[1024,16]{0,1:T(8,128)}, u32[]{:S(2)}) copy-start(f32[1024,16]{0,1:T(8,128)} %param.10) | copy-start | bytes 196612
  52.4 0.7 copy-start.7
  53.0 46.9 %copy-start.1 = (bf16[3,128,1024]{2,1,0:T(8,128)(2,1)S(1)}, bf16[3,128,1024]{2,1,0:T(8,128)(2,1)}, u32[]{:S(2)}) copy-start(bf16[3,128,1024]{2,1,0:T(8,128)(2,1)} %streams.3) | copy-start | bytes 2359300
  78.2 21.7 %copy-start.3 = (bf16[128,1024]{1,0:T(8,128)(2,1)S(1)}, bf16[128,1024]{1,0:T(8,128)(2,1)}, u32[]{:S(2)}) copy-start(bf16[128,1024]{1,0:T(8,128)(2,1)} %cotangent.3) | copy-start | bytes 786436
where the time goes:
time: 119 us; the launch traced here: 118 us
  blocking collectives  79.9 us (67%)
  Pallas kernels  33.4 us (28%)
  local copies, waits for them, and re-layouts  2.75 us (2%)
  between operations  1.37 us (1%)
    all_to_all x1, blocking collectives, body(): lax.all_to_all(turned, 'ctx', split_axis=0, concat_axis=0, tiled=True)  49.3 us
    pallas_call x1, Pallas kernels, body(): pl.pallas_call(functools.partial(owner_kernel, total), out_shape=jax.Shap...  25.2 us
    all_to_all x1, blocking collectives, body(): lax.all_to_all(payload.reshape(shards, OWN, LANES), 'ctx', split_axis=0,...  21.7 us
    psum x1, blocking collectives, body(): squares = lax.psum(squares[0, 0], 'ch')  8.95 us
    pallas_call x1, Pallas kernels, body(): pl.pallas_call(functools.partial(shard_kernel, total), out_shape=[jax.Sha...  7.84 us
    unnamed x16, local copies, waits for them, and re-layouts  2.75 us

commit v1 on v0

v1 whole, which is shorter than its diff:
```python
import functools

import jax
import jax.numpy as jnp
from jax import lax
from jax.experimental import pallas as pl
from jax.experimental.pallas import tpu as pltpu
from jax.sharding import PartitionSpec as P

F32 = jnp.float32
BF16 = jnp.bfloat16
TAPS = 7
REACH = TAPS - 1
TOK = 128
LANES = 128
OWN = 8
SUB = 8
GROUP = 8
STAGE = 99

LEFT = LANES - 3 * REACH
RIGHT = 0
STATE = 18
MODES = 16
GRADS = STATE + 4 * MODES


def rounded(value):
    return value.astype(BF16).astype(F32)


def halves(value):
    high = value.astype(BF16)
    return high, (value - high.astype(F32)).astype(BF16)


def one_minus_exp(x):
    series = jnp.full_like(x, 1.0)
    for n in range(11, 1, -1):
        series = 1.0 - (x * F32(1.0 / n)) * series
    return x * series


def gains(rate, gain):
    return gain * jnp.sqrt(one_minus_exp(2.0 * rate))


def start_list(seq_ref):
    starts = [jnp.int32(0)]
    for n in range(seq_ref.shape[0]):
        starts.append(starts[-1] + seq_ref[n])
    return starts


def dot(a, b):
    return lax.dot_general(a, b, (((1,), (0,)), ((), ())), preferred_element_type=F32)


def dot_t(a, b):
    return lax.dot_general(a, b, (((1,), (1,)), ((), ())), preferred_element_type=F32)


def turn_kernel(streams, cotangent, out):
    for pair in range(2):
        for k in range(SUB):
            cols = pl.ds(k * LANES, LANES)
            first = streams[2 * pair, :, cols]
            second = streams[1, :, cols] if pair == 0 else cotangent[:, cols]
            a = first.astype(F32).T.reshape(LANES // OWN, OWN, TOK)
            b = second.astype(F32).T.reshape(LANES // OWN, OWN, TOK)
            out[pl.ds(k * (LANES // OWN), LANES // OWN), pl.ds(pair * 16, 16), :] = (
                jnp.concatenate([a, b], axis=1).astype(BF16)
            )


ROWS_OF = (0, 8, 16, 24)


def owner_kernel(
    total, seq, moved, weight, rate, gain, out, sh, wide, u, dz, kc, vc, zs, ds, pay, halos, fixf, fixb, prm
):
    blocks = moved.shape[0]
    index = lax.axis_index("ctx")
    starts = start_list(seq)
    starts[-1] = jnp.int32(total)
    nseq = seq.shape[0]
    lane = lax.broadcasted_iota(jnp.int32, (SUB, LANES), 1)

    chunk = pl.multiple_of((index // (LANES // OWN)) * LANES, LANES)
    back = lax.rem(LANES - lax.rem(index, LANES // OWN) * OWN, LANES)
    cols = pl.ds(chunk, LANES)
    prm[...] = jnp.zeros_like(prm)
    prm[0:MODES, :] = pltpu.roll(rate[:, cols], back, 1)
    prm[MODES : 2 * MODES, :] = pltpu.roll(gain[:, cols], back, 1)
    for i in range(3):
        prm[32 + 8 * i : 32 + 8 * i + TAPS, :] = weight[i, :, cols]
    prm[32:56, :] = pltpu.roll(prm[32:56, :], back, 1)
    own = prm[...].T[0:OWN, :]
    for i in range(3):
        for j in range(TAPS):
            f = 32 + 8 * i + j
            wide[i * TAPS + j] = jnp.broadcast_to(own[:, f : f + 1], (SUB, LANES))
    rate_rows = jnp.concatenate(
        [jnp.broadcast_to(own[:, m : m + 1], (SUB, LANES)) for m in range(MODES)], axis=0
    )
    gain_rows = jnp.concatenate(
        [
            jnp.broadcast_to(own[:, MODES + m : MODES + m + 1], (SUB, LANES))
            for m in range(MODES)
        ],
        axis=0,
    )
    coef_rows = gains(rate_rows, gain_rows)

    def filtering(b, now, before, since):
        done = []
        for i in range(3):
            x = now[ROWS_OF[i] : ROWS_OF[i] + 8]
            p = before[ROWS_OF[i] : ROWS_OF[i] + 8]
            acc = wide[i * TAPS] * x
            for j in range(1, TAPS):
                moved_x = pltpu.roll(jnp.where(lane >= LANES - j, p, x), j, 1)
                if since is not None:
                    moved_x = jnp.where(since >= j, moved_x, 0.0)
                sh[i * REACH + j - 1, b] = moved_x
                acc = acc + wide[i * TAPS + j] * moved_x
            done.append(acc)
        rows = pl.ds(pl.multiple_of(b * SUB, SUB), SUB)
        u[rows, :] = rounded(done[1] * done[2])
        dz[rows, :] = rounded(now[24:32] * done[0])
        kc[rows, :] = done[1]
        vc[rows, :] = done[2]

    def filter_group(n, _):
        b0 = n * GROUP
        held = [moved[jnp.maximum(b0 - 1, 0)].astype(F32)]
        held += [moved[b0 + g].astype(F32) for g in range(GROUP)]
        for g in range(GROUP):
            filtering(b0 + g, held[g + 1], held[g], None)
        return 0

    lax.fori_loop(0, blocks // GROUP, filter_group, 0)
    if STAGE < 2:
        return
    for s in starts[:-1]:
        for near in (0, 1):
            b = jnp.minimum(s // TOK + near, blocks - 1)
            place = b * TOK + lane
            since = jnp.zeros((SUB, LANES), jnp.int32)
            for other in starts[:-1]:
                since = jnp.where(other <= place, other, since)
            filtering(
                b,
                moved[b].astype(F32),
                moved[jnp.maximum(b - 1, 0)].astype(F32),
                place - since,
            )

    for n in range(nseq):
        b = starts[n] // TOK
        rows = pl.ds(pl.multiple_of(b * SUB, SUB), SUB)
        place = b * TOK + lane
        fixf[n * SUB : (n + 1) * SUB, :] = jnp.where(place >= starts[n], u[rows, :], 0.0)
        fixb[n * SUB : (n + 1) * SUB, :] = jnp.where(place < starts[n], dz[rows, :], 0.0)
    if STAGE < 3:
        return

    row = lax.broadcasted_iota(jnp.int32, (blocks, TOK), 0)
    col = lax.broadcasted_iota(jnp.int32, (blocks, TOK), 1)
    head = jnp.ones((blocks, TOK), F32)
    tail = jnp.ones((blocks, TOK), F32)
    spot = row * TOK + col
    for s in starts[:-1]:
        base = s - lax.rem(s, TOK)
        head = jnp.where((spot >= s) & (spot < base + TOK), 0.0, head)
        tail = jnp.where((spot < s) & (spot >= base), 0.0, tail)

    lag = col.astype(F32)
    ending = halves(jnp.exp(-rate_rows * (TOK - 1.0 - lag)))
    falling = jnp.exp(-rate_rows * lag)
    opening = halves(falling)
    lead_f = halves(coef_rows * jnp.exp(-rate_rows * (lag + 1.0)))
    lead_b = halves(coef_rows * jnp.exp(-rate_rows * (TOK - lag)))
    whole = jnp.exp(-rate_rows * TOK).T[0:1, :]
    taps = (coef_rows * falling).reshape(MODES, OWN, LANES).sum(axis=0)

    mine = lax.rem(col, OWN)
    ending = jnp.concatenate(ending, axis=1)
    opening = jnp.concatenate(opening, axis=1)
    end_f = jnp.zeros((blocks, LANES), F32)
    end_b = jnp.zeros((blocks, LANES), F32)
    if STAGE < 4:
        zs[0:LANES, :] = head + tail + whole + lead_f[0].astype(F32) + lead_b[0].astype(F32)
        zs[0:LANES, :] = ending[:, :LANES].astype(F32) + opening[:, :LANES].astype(F32)
        zs[0:8, :] = taps
        return
    for c in range(OWN):
        uc = (u[pl.ds(c, blocks, stride=OWN), :] * tail).astype(BF16)
        dc = (dz[pl.ds(c, blocks, stride=OWN), :] * head).astype(BF16)
        ef = dot_t(jnp.concatenate([uc, uc], axis=1), ending)
        eb = dot_t(jnp.concatenate([dc, dc], axis=1), opening)
        end_f = jnp.where(mine == c, ef, end_f)
        end_b = jnp.where(mine == c, eb, end_b)
    if STAGE < 5:
        zs[0:LANES, :] = end_f + end_b
        return

    keep_f = head[:, TOK - 1 : TOK] * whole
    keep_b = keep_f
    step = 1
    while step < blocks:
        low = row >= step
        end_f = end_f + jnp.where(low, keep_f * pltpu.roll(end_f, step, 0), 0.0)
        keep_f = jnp.where(low, keep_f * pltpu.roll(keep_f, step, 0), 0.0)
        high = row < blocks - step
        end_b = end_b + jnp.where(high, keep_b * pltpu.roll(end_b, blocks - step, 0), 0.0)
        keep_b = jnp.where(high, keep_b * pltpu.roll(keep_b, blocks - step, 0), 0.0)
        step *= 2
    state_f = jnp.where(row >= 1, pltpu.roll(end_f, 1, 0), 0.0)
    state_b = jnp.where(row < blocks - 1, pltpu.roll(end_b, blocks - 1, 0), 0.0)
    sf = halves(state_f)
    sb = halves(state_b)
    if STAGE < 6:
        zs[0:LANES, :] = sf[0].astype(F32) + sf[1].astype(F32)
        zs[0:LANES, :] = sb[0].astype(F32) + sb[1].astype(F32)
        return

    zero = jnp.zeros((blocks, LANES), BF16)
    every = jnp.concatenate([sf[0], sf[1], sb[0], sb[1]], axis=1)
    pick_row = lax.broadcasted_iota(jnp.int32, (4 * LANES, LANES), 0)
    pick_col = lax.broadcasted_iota(jnp.int32, (4 * LANES, LANES), 1)
    target = STATE + (pick_row // LANES) * MODES + lax.rem(pick_row, LANES) // OWN
    lands = pick_col == target
    pick_mine = lax.rem(pick_row, OWN)
    for c in range(OWN):
        strip = jnp.broadcast_to(taps[c : c + 1, :], (LANES, LANES))
        strip = pltpu.roll(strip, 0, 1, stride=1, stride_axis=0)
        strip = jnp.where(col >= row, strip, 0.0)
        kern = halves(strip)
        nrek = halves(strip.T)
        of_c = mine == c
        uc = u[pl.ds(c, blocks, stride=OWN), :].astype(BF16)
        dc = dz[pl.ds(c, blocks, stride=OWN), :].astype(BF16)
        fh, fl = [jnp.where(of_c, x, zero) for x in sf]
        bh, bl = [jnp.where(of_c, x, zero) for x in sb]
        both = jnp.concatenate([uc, fh], axis=1)
        zc = dot(both, jnp.concatenate([kern[0], lead_f[0]], axis=0))
        zc = zc + dot(both, jnp.concatenate([kern[1], lead_f[1]], axis=0))
        zs[pl.ds(c, blocks, stride=OWN), :] = zc + dot(fl, lead_f[0])
        both = jnp.concatenate([dc, bh], axis=1)
        rc = dot(both, jnp.concatenate([nrek[0], lead_b[0]], axis=0))
        rc = rc + dot(both, jnp.concatenate([nrek[1], lead_b[1]], axis=0))
        ds[pl.ds(c, blocks, stride=OWN), :] = rc + dot(bl, lead_b[0])
        few = fixf[pl.ds(c, nseq, stride=OWN), :].astype(BF16)
        fixf[pl.ds(c, nseq, stride=OWN), :] = dot(few, kern[0]) + dot(few, kern[1])
        few = fixb[pl.ds(c, nseq, stride=OWN), :].astype(BF16)
        fixb[pl.ds(c, nseq, stride=OWN), :] = dot(few, nrek[0]) + dot(few, nrek[1])
        pick = jnp.where(lands & (pick_mine == c), 1.0, 0.0).astype(BF16)
        pay[pl.ds(c, blocks, stride=OWN), :] = dot(every, pick)
    if STAGE < 7:
        return
    for n in range(nseq):
        b = starts[n] // TOK
        rows = pl.ds(pl.multiple_of(b * SUB, SUB), SUB)
        place = b * TOK + lane
        fresh = (place >= starts[n]) & (place < starts[n + 1])
        zs[rows, :] = jnp.where(fresh, fixf[n * SUB : (n + 1) * SUB, :], zs[rows, :])
        if n > 0:
            fresh = (place >= starts[n - 1]) & (place < starts[n])
            ds[rows, :] = jnp.where(fresh, fixb[n * SUB : (n + 1) * SUB, :], ds[rows, :])
    if STAGE < 8:
        return

    def gradient_group(n, acc):
        acc = list(acc)
        for g in range(GROUP):
            b = n * GROUP + g
            rows = pl.ds(pl.multiple_of(b * SUB, SUB), SUB)
            now = moved[b].astype(F32)
            z = rounded(zs[rows, :])
            d = rounded(ds[rows, :])
            df = (now[24:32] * z, d * vc[rows, :], d * kc[rows, :])
            for i in range(3):
                f = i * TAPS
                acc[f] = acc[f] + df[i] * now[ROWS_OF[i] : ROWS_OF[i] + 8]
                for j in range(1, TAPS):
                    acc[f + j] = acc[f + j] + df[i] * sh[i * REACH + j - 1, b]
            halo = jnp.where(lane < REACH, df[0], 0.0)
            for i in (1, 2):
                part = pltpu.roll(df[i], i * REACH, 1)
                halo = jnp.where((lane >= i * REACH) & (lane < (i + 1) * REACH), part, halo)
            halos[rows, :] = halo
        return tuple(acc)

    acc = lax.fori_loop(
        0,
        blocks // GROUP,
        gradient_group,
        tuple(jnp.zeros((SUB, LANES), F32) for _ in range(3 * TAPS)),
    )
    grads = jnp.zeros((SUB, LANES), F32)
    for f in range(3 * TAPS):
        grads = jnp.where(lane == GRADS + f, jnp.sum(acc[f], axis=1, keepdims=True), grads)
    if STAGE < 9:
        zs[0:8, :] = grads
        return

    def finish_group(n, _):
        b0 = n * GROUP
        held = [moved[jnp.maximum(b0 - 1, 0)].astype(F32)]
        held += [moved[b0 + g].astype(F32) for g in range(GROUP - 1)]
        tiles = []
        for g in range(GROUP):
            b = b0 + g
            after = jnp.minimum(b + 1, blocks - 1)
            value = pay[pl.ds(pl.multiple_of(b * SUB, SUB), SUB), :] + grads
            value = value + halos[pl.ds(pl.multiple_of(after * SUB, SUB), SUB), :]
            for i in range(3):
                x = held[g][ROWS_OF[i] : ROWS_OF[i] + 8]
                first = LEFT + i * REACH
                x = x if i == 2 else pltpu.roll(x, first - (TOK - REACH) + LANES, 1)
                value = jnp.where((lane >= first) & (lane < first + REACH), x, value)
            tiles.append(value)
        for g in range(0, GROUP, 2):
            rows = pl.ds(pl.multiple_of((b0 + g) * SUB, 16), 16)
            out[rows, :] = jnp.concatenate(tiles[g : g + 2], axis=0).astype(BF16)
        return 0

    lax.fori_loop(0, blocks // GROUP, finish_group, 0)


def put(ref, t, value):
    ref[pl.ds(pl.multiple_of(t * SUB, SUB), SUB), :] = value


def at(ref, t):
    return ref[pl.ds(pl.multiple_of(t * SUB, SUB), SUB), :]


def put3(ref, i, t, value):
    ref[i, pl.ds(pl.multiple_of(t * SUB, SUB), SUB), :] = value


def at3(ref, i, t):
    return ref[i, pl.ds(pl.multiple_of(t * SUB, SUB), SUB), :]


def tile(ref, n):
    return ref[pl.ds(n * SUB, SUB), :]


def local_starts(total, seq):
    index = lax.axis_index("ctx")
    local = [s - index * TOK for s in start_list(seq)]
    local[-1] = total - index * TOK
    return local


def since(local, t):
    last = local[0]
    for s in local[1:]:
        last = jnp.where(s <= t, s, last)
    return t - last


def until(local, t):
    following = local[-1]
    for s in local[-2::-1]:
        following = jnp.where(s > t, s, following)
    return following - t


def near(local, t0):
    found = jnp.bool_(False)
    for s in local:
        found = found | ((s >= t0 - REACH) & (s < t0 + 8 + REACH + 1))
    return found


def eight_filtered(local, xs, ws, base, t0, masked):
    ages = [since(local, t0 + r) for r in range(8)] if masked else None
    done = []
    for i in range(3):
        w = [tile(ws, i * 8 + j) for j in range(TAPS)]
        x = [at3(xs, i, t0 + base - REACH + n) for n in range(8 + REACH)]
        row = []
        for r in range(8):
            acc = w[0] * x[r + REACH]
            for j in range(1, TAPS):
                term = w[j] * x[r + REACH - j]
                if masked:
                    term = jnp.where(ages[r] >= j, term, 0.0)
                acc = acc + term
            row.append(acc)
        done.append(row)
    return done


def prepare_kernel(
    total, seq, streams, cotangent, weight, rate, gain, qs, ks, vs, cots, heads, ws, prm, xs
):
    local = local_starts(total, seq)
    for k in range(SUB):
        cols = pl.ds(k * LANES, LANES)
        for g in range(MODES // 8):
            r = rate[g * 8 : g * 8 + 8, cols]
            prm[pl.ds(g * 64 + k, 8, stride=SUB), :] = jnp.exp(-r)
            prm[pl.ds(MODES * SUB + g * 64 + k, 8, stride=SUB), :] = gains(
                r, gain[g * 8 : g * 8 + 8, cols]
            )
        for i in range(3):
            ws[pl.ds(i * 64 + k, TAPS, stride=SUB), :] = weight[i, :, cols]
        for g in range(TOK // 16):
            some = pl.ds(g * 16, 16)
            for i in range(4):
                x = streams[i, some, cols] if i < 3 else cotangent[some, cols]
                x = x.astype(F32)
                for h in range(2):
                    rows = pl.ds((g * 16 + h * 8) * SUB + k, 8, stride=SUB)
                    part = x[h * 8 : h * 8 + 8]
                    if i == 3:
                        cots[rows, :] = part
                    else:
                        xs[i, rows, :] = part
                        if g == 0 and h == 0:
                            heads[i, rows, :] = part

    def filtering(t0, masked):
        done = eight_filtered(local, xs, ws, 0, t0, masked)
        for r in range(8):
            put(qs, t0 + r, done[0][r])
            put(ks, t0 + r, done[1][r])
            put(vs, t0 + r, done[2][r])

    def step(n, _):
        t0 = n * 8
        close = near(local, t0)

        @pl.when(close)
        def _():
            filtering(t0, True)

        @pl.when(jnp.logical_not(close))
        def _():
            filtering(t0, False)

        return 0

    lax.fori_loop(1, TOK // 8, step, 0)


def shard_kernel(
    total, seq, fields, qs, ks, vs, cots, heads, ws, prm, out, grads_out, wgrad,
    first, fs, q0, dzs, dfs, outs, sgs,
):
    local = local_starts(total, seq)
    for k in range(SUB):
        cols = pl.ds(k * LANES, LANES)
        turned = fields[pl.ds(k * LANES, LANES), :].astype(F32).T
        for g in range(LANES // 8):
            fs[pl.ds(g * 64 + k, 8, stride=SUB), :] = turned[g * 8 : g * 8 + 8]
    for i in range(3):
        first[i, 0 : REACH * SUB, :] = fs[(LEFT + i * REACH) * SUB : (LEFT + (i + 1) * REACH) * SUB, :]
        first[i, REACH * SUB : (REACH + 8) * SUB, :] = heads[i]
        dfs[i, TOK * SUB : (TOK + REACH) * SUB, :] = fs[
            (RIGHT + i * REACH) * SUB : (RIGHT + (i + 1) * REACH) * SUB, :
        ]
    done = eight_filtered(local, first, ws, REACH, 0, True)
    for i in range(3):
        for r in range(8):
            put3(q0, i, r, done[i][r])

    def forward(t0, state, masked, sources):
        q_ref, k_ref, v_ref = sources
        ages = [since(local, t0 + r) for r in range(8)] if masked else None
        state = list(state)
        for r in range(8):
            t = t0 + r
            q, c = at(q_ref, t), at(cots, t)
            put(dzs, t, rounded(c * q))
            u = rounded(at(k_ref, t) * at(v_ref, t))
            z = jnp.zeros((SUB, LANES), F32)
            for m in range(MODES):
                old = state[m]
                if masked:
                    old = jnp.where(ages[r] > 0, old, 0.0)
                state[m] = tile(prm, m) * old + u
                z = z + tile(prm, MODES + m) * state[m]
            z = rounded(z)
            put(outs, t, q * z)
            put3(dfs, 0, t, c * z)
        return tuple(state)

    def backward(t0, state, masked, sources):
        _, k_ref, v_ref = sources
        gaps = [until(local, t0 + r) for r in range(8)] if masked else None
        state = list(state)
        for r in range(7, -1, -1):
            t = t0 + r
            g = at(dzs, t)
            d = jnp.zeros((SUB, LANES), F32)
            for m in range(MODES):
                old = state[m]
                if masked:
                    old = jnp.where(gaps[r] > 1, old, 0.0)
                state[m] = tile(prm, m) * old + g
                d = d + tile(prm, MODES + m) * state[m]
            d = rounded(d)
            put3(dfs, 1, t, d * at(v_ref, t))
            put3(dfs, 2, t, d * at(k_ref, t))
        for i in range(3):
            w = [tile(ws, i * 8 + j) for j in range(TAPS)]
            y = [at3(dfs, i, t0 + n) for n in range(8 + REACH)]
            for r in range(8):
                acc = w[0] * y[r]
                for j in range(1, TAPS):
                    term = w[j] * y[r + j]
                    if masked:
                        term = jnp.where(gaps[r] > j, term, 0.0)
                    acc = acc + term
                put3(sgs, i, t0 + r, acc)
        return tuple(state)

    def entering(g):
        return tuple(
            tile(fs, STATE + g * MODES + m) + tile(fs, STATE + (g + 1) * MODES + m)
            for m in range(MODES)
        )

    edge = (q0.at[0], q0.at[1], q0.at[2])
    whole = (qs, ks, vs)

    def step_f(n, state):
        t0 = n * 8
        return lax.cond(
            near(local, t0),
            lambda s: forward(t0, s, True, whole),
            lambda s: forward(t0, s, False, whole),
            state,
        )

    def step_b(n, state):
        t0 = TOK - 8 - n * 8
        return lax.cond(
            near(local, t0),
            lambda s: backward(t0, s, True, whole),
            lambda s: backward(t0, s, False, whole),
            state,
        )

    state = forward(0, entering(0), True, edge)
    lax.fori_loop(1, TOK // 8, step_f, state)
    state = lax.fori_loop(0, TOK // 8 - 1, step_b, entering(2))
    backward(0, state, True, edge)

    for k in range(SUB):
        cols = pl.ds(k * LANES, LANES)
        for i in range(3):
            wgrad[i, :, cols] = fs[pl.ds((GRADS + i * TAPS) * SUB + k, TAPS, stride=SUB), :]
        for g in range(TOK // 16):
            for i in range(4):
                parts = []
                for h in range(2):
                    rows = pl.ds((g * 16 + h * 8) * SUB + k, 8, stride=SUB)
                    parts.append(sgs[i, rows, :] if i < 3 else outs[rows, :])
                both = jnp.concatenate(parts, axis=0).astype(BF16)
                if i < 3:
                    grads_out[i, pl.ds(g * 16, 16), cols] = both
                else:
                    out[pl.ds(g * 16, 16), cols] = both


def norm_kernel(fields, out):
    lane = lax.broadcasted_iota(jnp.int32, fields.shape, 1)
    value = fields[...].astype(F32)
    value = jnp.where((lane >= GRADS) & (lane < GRADS + 3 * TAPS), value, 0.0)
    out[...] = jnp.broadcast_to(jnp.sum(value * value), out.shape)


def clip_kernel(grads, squares, out):
    total = squares[0]
    for n in range(1, squares.shape[0]):
        total = total + squares[n]
    factor = jnp.minimum(F32(1.0), 1.0 / jnp.sqrt(total[0:1, :] + 1e-06))
    for k in range(grads.shape[2] // LANES):
        cols = pl.ds(k * LANES, LANES)
        for i in range(grads.shape[0]):
            out[i, :, cols] = grads[i, :, cols] * factor


def vmem():
    return pl.BlockSpec(memory_space=pltpu.VMEM)


def smem():
    return pl.BlockSpec(memory_space=pltpu.SMEM)


def body(streams, seq_lengths, conv_weight, rate, modal_gain, cotangent):
    tok, chans = streams.shape[1:]
    shards = lax.axis_size("ctx")
    total = tok * shards
    rate_t, gain_t = rate.T, modal_gain.T
    params = pltpu.CompilerParams(vmem_limit_bytes=48 * 1024 * 1024)
    turned = pl.pallas_call(
        turn_kernel,
        out_shape=jax.ShapeDtypeStruct((shards, 4 * OWN, tok), BF16),
        in_specs=[vmem()] * 2,
        out_specs=vmem(),
        compiler_params=params,
        name="turn",
    )(streams, cotangent)
    moved = lax.all_to_all(turned, "ctx", split_axis=0, concat_axis=0, tiled=True)
    plane = jax.ShapeDtypeStruct((tok * SUB, LANES), F32)
    prepared = pl.pallas_call(
        functools.partial(prepare_kernel, total),
        out_shape=[plane] * 4
        + [
            jax.ShapeDtypeStruct((3, 8 * SUB, LANES), F32),
            jax.ShapeDtypeStruct((3 * 8 * SUB, LANES), F32),
            jax.ShapeDtypeStruct((2 * MODES * SUB, LANES), F32),
        ],
        in_specs=[smem()] + [vmem()] * 5,
        out_specs=[vmem()] * 7,
        scratch_shapes=[pltpu.VMEM((3, tok * SUB, LANES), F32)],
        compiler_params=params,
        cost_estimate=pl.CostEstimate(flops=20_000_000, bytes_accessed=4_000_000, transcendentals=0),
        name="prepare",
    )(seq_lengths, streams, cotangent, conv_weight, rate_t, gain_t)
    moved, *prepared = lax.optimization_barrier((moved, *prepared))
    rows = shards * OWN
    plane = pltpu.VMEM((rows, LANES), F32)
    payload = pl.pallas_call(
        functools.partial(owner_kernel, total),
        out_shape=jax.ShapeDtypeStruct((rows, LANES), BF16),
        in_specs=[smem()] + [vmem()] * 4,
        out_specs=vmem(),
        scratch_shapes=[
            pltpu.VMEM((3 * REACH, shards, SUB, LANES), F32),
            pltpu.VMEM((3 * TAPS, SUB, LANES), F32),
        ]
        + [plane] * 8
        + [pltpu.VMEM((8 * SUB, LANES), F32)] * 2
        + [pltpu.VMEM((LANES, LANES), F32)],
        compiler_params=params,
        name="owner",
    )(seq_lengths, moved, conv_weight, rate_t, gain_t)
    fields = lax.all_to_all(
        payload.reshape(shards, OWN, LANES), "ctx", split_axis=0, concat_axis=0, tiled=True
    ).reshape(rows, LANES)
    planes = lax.axis_size("ch")
    partial = pl.pallas_call(
        norm_kernel,
        out_shape=jax.ShapeDtypeStruct((planes, SUB, LANES), F32),
        in_specs=[vmem()],
        out_specs=vmem(),
        name="norm",
    )(fields)
    squares = lax.all_to_all(partial, "ch", split_axis=0, concat_axis=0, tiled=True)
    scratch = pltpu.VMEM((tok * SUB, LANES), F32)
    output, stream_grads, weight_grad = pl.pallas_call(
        functools.partial(shard_kernel, total),
        out_shape=[
            jax.ShapeDtypeStruct((tok, chans), BF16),
            jax.ShapeDtypeStruct((3, tok, chans), BF16),
            jax.ShapeDtypeStruct((3, TAPS, chans), F32),
        ],
        in_specs=[smem()] + [vmem()] * 8,
        out_specs=[vmem()] * 3,
        scratch_shapes=[
            pltpu.VMEM((3, (REACH + 8) * SUB, LANES), F32),
            pltpu.VMEM((LANES * SUB, LANES), F32),
            pltpu.VMEM((3, 8 * SUB, LANES), F32),
            scratch,
            pltpu.VMEM((3, (tok + REACH) * SUB, LANES), F32),
            scratch,
            pltpu.VMEM((3, tok * SUB, LANES), F32),
        ],
        compiler_params=params,
        cost_estimate=pl.CostEstimate(flops=40_000_000, bytes_accessed=6_000_000, transcendentals=0),
        name="shard",
    )(seq_lengths, fields, *prepared)
    clipped = pl.pallas_call(
        clip_kernel,
        out_shape=jax.ShapeDtypeStruct(weight_grad.shape, F32),
        in_specs=[vmem()] * 2,
        out_specs=vmem(),
        name="clip",
    )(weight_grad, squares)
    return output, stream_grads, clipped


def solution(mesh):
    return jax.shard_map(
        body,
        mesh=mesh,
        in_specs=(
            P(None, "ctx", "ch"),
            P(),
            P(None, None, "ch"),
            P("ch", None),
            P("ch", None),
            P("ctx", "ch"),
        ),
        out_specs=(P("ctx", "ch"), P(None, "ctx", "ch"), P(None, None, "ch")),
        check_vma=False,
    )
```

time: 119 us -> 101 us (0.85)
  blocking collectives: 79.9 us -> 21.8 us
  waiting for transfers between devices: 0 us -> 25.1 us
  starting transfers between devices: 0 us -> 22.6 us
  Pallas kernels: 33.4 us -> 23.1 us
  local copies, waits for them, and re-layouts: 2.75 us -> 6.82 us
    all_to_all x1 -> x0, blocking collectives: 49.3 us -> none  [body(): lax.all_to_all(turned, 'ctx', split_axis=0, concat_axis=0, tiled=True)]
    all_to_all x0 -> x2, waiting for transfers between devices: none -> 25.1 us  [the longest x1 25.1 us: body(): lax.all_to_all(turned, 'ctx', split_axis=0, concat_axis=0, tiled=True)]
    all_to_all x0 -> x2, starting transfers between devices: none -> 22.6 us  [the longest x1 18.6 us: body(): lax.all_to_all(turned, 'ctx', split_axis=0, concat_axis=0, tiled=True)]
    pallas_call x1, Pallas kernels: 25.2 us -> 9.29 us  [body(): pl.pallas_call(functools.partial(owner_kernel, total), out_shape=jax.Shap...]
    psum x1 -> x0, blocking collectives: 8.95 us -> none  [body(): squares = lax.psum(squares[0, 0], 'ch')]
    pallas_call x0 -> x3, Pallas kernels: none -> 5.71 us  [the longest x1 2.28 us: body(): pl.pallas_call(functools.partial(prepare_kernel, total), out_shape=[plane...]
    unnamed x16 -> x38, local copies, waits for them, and re-layouts: 2.75 us -> 6.82 us
  transfers between devices with their start and end apart: 0 -> 2, of which waited for: 0 -> 1; matrix products, arithmetic and copies ran while one was open for 0% -> 0% of each run, Pallas kernels for 0% -> 9%
where the time goes in v1:
time: 101 us; the launch traced here: 100 us
  waiting for transfers between devices  25.1 us (25%)
  Pallas kernels  23.1 us (23%)
  starting transfers between devices  22.6 us (22%)
  blocking collectives  21.8 us (22%)
  local copies, waits for them, and re-layouts  6.82 us (7%)
    all_to_all x1, waiting for transfers between devices, body(): lax.all_to_all(turned, 'ctx', split_axis=0, concat_axis=0, tiled=True)  25.1 us
    all_to_all x1, blocking collectives, body(): lax.all_to_all(payload.reshape(shards, OWN, LANES), 'ctx', split_axis=0,...  21.8 us
    all_to_all x1, starting transfers between devices, body(): lax.all_to_all(turned, 'ctx', split_axis=0, concat_axis=0, tiled=True)  18.6 us
    pallas_call x1, Pallas kernels, body(): pl.pallas_call(functools.partial(owner_kernel, total), out_shape=jax.Shap...  9.29 us
    unnamed x38, local copies, waits for them, and re-layouts  6.82 us
    pallas_call x1, Pallas kernels, body(): pl.pallas_call(functools.partial(shard_kernel, total), out_shape=[jax.Sha...  6.73 us
    all_to_all x1, starting transfers between devices, body(): lax.all_to_all(partial, 'ch', split_axis=0, concat_axis=0, tiled=True)  4.01 us
    pallas_call x1, Pallas kernels, body(): pl.pallas_call(functools.partial(prepare_kernel, total), out_shape=[plane...  2.28 us
  transfers between devices with their start and end apart: 2, of which 1 were waited for; matrix products, arithmetic and copies ran while one was open for 0% of the time, Pallas kernels for 9%

profile of v1, /device:TPU:1, one launch (start us, length us, event | category | flops | bytes accessed | tf_op | source)
XLA Modules:
  0.0 100.1 jit_solution(622704377537309161)
XLA Ops:
  0.6 0.0 copy-start
  0.6 1.1 %copy-done = bf16[3,128,1024]{2,1,0:T(8,128)(2,1)S(1)} copy-done((bf16[3,128,1024]{2,1,0:T(8,128)(2,1)S(1)}, bf16[3,128,1024]{2,1,0:T(8,128)(2,1)}, u32[]{:S(2)}) %copy-start) | copy-done | bytes 786456
  1.8 0.0 copy-start.3
  1.8 0.9 copy-done.3
  2.7 1.3 %turn.1 = bf16[128,32,128]{2,1,0:T(8,128)(2,1)} custom-call(bf16[3,128,1024]{2,1,0:T(8,128)(2,1)S(1)} %copy-done, bf16[128,1024]{1,0:T(8,128)(2,1)S(1)} %copy-done.3), custom_call_target="tpu_custom_call" | custom-call | tf_op jit(solution)/shard_map/turn/pallas_call | solution.py:605
  4.0 0.0 copy-start.1
  4.1 0.0 copy-start.4
  4.1 0.0 copy-start.9
  4.1 0.0 copy-start.10
  4.1 0.0 copy-start.11
  4.1 18.6 %all-to-all-start = ((bf16[128,32,128]{2,1,0:T(8,128)(2,1)}), bf16[128,32,128]{2,1,0:T(8,128)(2,1)S(1)}, u32[]{:S(2)}, u32[]{:S(2)}) async-start(bf16[128,32,128]{2,1,0:T(8,128)(2,1)} %turn.1), calls=%async_computation | async-start | bytes 2097152 | tf_op jit(solution)/shard_map/all_to_all | solution.py:613
  22.6 0.0 copy-start.17
  22.7 0.0 copy-done.1
  22.7 0.0 copy-done.4
  22.7 0.0 copy-done.9
  22.7 0.0 copy-done.10
  22.7 0.0 copy-done.11
  22.7 0.6 copy-done.17
  23.3 2.3 %prepare.1 = (f32[1024,128]{1,0:T(8,128)S(1)}, f32[1024,128]{1,0:T(8,128)S(1)}, f32[1024,128]{1,0:T(8,128)S(1)}, f32[1024,128]{1,0:T(8,128)S(1)}, f32[3,64,128]{...) custom-call(s32[8]{0:T(128)S(1)} %copy-done.17, bf16[3,128,1024]{2,1,0:T(8,128)(2,1)S(1)} %copy-done.1, ...), custom_call_target="tpu_custom_call" | custom-call | flops 20000000 | bytes 4000000 | tf_op jit(solution)/shard_map/prepare/pallas_call | solution.py:615
  25.6 0.0 copy-start.5
  25.6 0.8 copy-done.5
  26.4 0.0 copy-start.7
  26.4 0.8 copy-done.7
  27.2 0.0 copy-start.12
  27.2 0.6 copy-done.12
  27.8 0.0 copy-start.14
  27.8 0.6 copy-done.14
  28.5 25.1 %all-to-all-done.moved = bf16[128,32,128]{2,1,0:T(8,128)(2,1)S(1)} async-done(((bf16[128,32,128]{2,1,0:T(8,128)(2,1)}), bf16[128,32,128]{2,1,0:T(8,128)(2,1)S(1)}, u32[]{:S(2)}, u32[]{:S(2)}) %all-to-all-start) | async-done | bytes 1048608 | tf_op jit(solution)/shard_map/all_to_all | solution.py:613
  53.5 0.0 copy-start.8
  53.5 0.0 copy-start.13
  53.6 0.0 copy-start.15
  53.6 9.3 %owner.1 = bf16[1024,128]{1,0:T(8,128)(2,1)S(1)} custom-call(s32[8]{0:T(128)S(1)} %copy-done.17, bf16[128,32,128]{2,1,0:T(8,128)(2,1)S(1)} %all-to-all-done.moved, f32[3,7,1024]{2,1,0:T(8,128)S(1)} %copy-done.9, f32[16,1024]{1,0:T(8,128)S(1)} %bitcast.8, f32[16,1024]{1,0:T(8,128)S(1)} %bitcast.10), custom_call_target="tpu_custom_call" | custom-call | tf_op jit(solution)/shard_map/owner/pallas_call | solution.py:633
  62.8 0.0 copy-start.6
  62.9 21.8 %all_to_all.15 = bf16[128,8,128]{2,1,0:T(8,128)(2,1)} all-to-all(bf16[128,8,128]{2,1,0:T(8,128)(2,1)S(1)} %bitcast.6), channel_id=1, replica_groups=mesh['ctx'=128,'ch'=4] {'ctx'}, dimensions={0} | all-to-all | bytes 524288 | tf_op jit(solution)/shard_map/all_to_all | solution.py:648
  84.6 0.0 copy-start.2
  84.6 1.9 %norm.1 = f32[4,8,128]{2,1,0:T(8,128)} custom-call(bf16[1024,128]{1,0:T(8,128)(2,1)} %bitcast.4), custom_call_target="tpu_custom_call" | custom-call | tf_op jit(solution)/shard_map/norm/pallas_call | solution.py:652
  86.5 4.0 %all-to-all-start.2 = ((f32[4,8,128]{2,1,0:T(8,128)}), f32[4,8,128]{2,1,0:T(8,128)S(1)}, u32[]{:S(2)}, u32[]{:S(2)}) async-start(f32[4,8,128]{2,1,0:T(8,128)} %norm.1), calls=%async_computation.2 | async-start | bytes 32768 | tf_op jit(solution)/shard_map/all_to_all | solution.py:659
  90.5 0.0 copy-done.8
  90.5 0.0 copy-done.13
  90.5 0.0 copy-done.15
  90.5 0.0 copy-done.6
  90.5 0.0 copy-done.2
  90.6 6.7 %shard.1 = (bf16[128,1024]{1,0:T(8,128)(2,1)}, bf16[3,128,1024]{2,1,0:T(8,128)(2,1)}, f32[3,7,1024]{2,1,0:T(8,128)S(1)}) custom-call(s32[8]{0:T(128)S(1)} %copy-done.17, bf16[1024,128]{1,0:T(8,128)(2,1)S(1)} %bitcast.5, f32[1024,128]{1,0:T(8,128)S(1)} %get-tuple-element.29.qs, f32[1024,128]{1,0:T(8,128)S(1)} %get-tuple-element.30.ks, ...), custom_call_target="tpu_custom_call" | custom-call | flops 40000000 | bytes 6000000 | tf_op jit(solution)/shard_map/shard/pallas_call | solution.py:661
  97.3 0.0 copy-start.16
  97.3 0.6 copy-done.16
  97.9 0.0 all-to-all-done.2.squares
  97.9 0.6 copy-done.18
  98.5 1.6 %clip.1 = f32[3,7,1024]{2,1,0:T(8,128)} custom-call(f32[3,7,1024]{2,1,0:T(8,128)} %copy-done.16, f32[4,8,128]{2,1,0:T(8,128)} %copy-done.18), custom_call_target="tpu_custom_call" | custom-call | tf_op jit(solution)/shard_map/clip/pallas_call | solution.py:683
  (1 shorter events, 0.0 us)
Async XLA Ops:
  0.6 1.1 %copy-start = (bf16[3,128,1024]{2,1,0:T(8,128)(2,1)S(1)}, bf16[3,128,1024]{2,1,0:T(8,128)(2,1)}, u32[]{:S(2)}) copy-start(bf16[3,128,1024]{2,1,0:T(8,128)(2,1)} %streams.3) | copy-start | bytes 2359300
  1.8 0.9 copy-start.3
  4.0 18.6 %copy-start.1 = (bf16[3,128,1024]{2,1,0:T(8,128)(2,1)S(1)}, bf16[3,128,1024]{2,1,0:T(8,128)(2,1)}, u32[]{:S(2)}) copy-start(bf16[3,128,1024]{2,1,0:T(8,128)(2,1)} %streams.3) | copy-start | bytes 2359300
  4.1 18.6 %copy-start.4 = (bf16[128,1024]{1,0:T(8,128)(2,1)S(1)}, bf16[128,1024]{1,0:T(8,128)(2,1)}, u32[]{:S(2)}) copy-start(bf16[128,1024]{1,0:T(8,128)(2,1)} %cotangent.3) | copy-start | bytes 786436
  4.1 18.6 %copy-start.9 = (f32[3,7,1024]{2,1,0:T(8,128)S(1)}, f32[3,7,1024]{2,1,0:T(8,128)}, u32[]{:S(2)}) copy-start(f32[3,7,1024]{2,1,0:T(8,128)} %weight.3) | copy-start | bytes 258052
  4.1 18.6 %copy-start.10 = (f32[1024,16]{0,1:T(8,128)S(1)}, f32[1024,16]{0,1:T(8,128)}, u32[]{:S(2)}) copy-start(f32[1024,16]{0,1:T(8,128)} %param.9) | copy-start | bytes 196612
  4.1 18.6 %copy-start.11 = (f32[1024,16]{0,1:T(8,128)S(1)}, f32[1024,16]{0,1:T(8,128)}, u32[]{:S(2)}) copy-start(f32[1024,16]{0,1:T(8,128)} %param.10) | copy-start | bytes 196612
  4.1 49.5 %all-to-all-start = ((bf16[128,32,128]{2,1,0:T(8,128)(2,1)}), bf16[128,32,128]{2,1,0:T(8,128)(2,1)S(1)}, u32[]{:S(2)}, u32[]{:S(2)}) async-start(bf16[128,32,128]{2,1,0:T(8,128)(2,1)} %turn.1), calls=%async_computation | async-start | bytes 2097152 | tf_op jit(solution)/shard_map/all_to_all | solution.py:613
  22.6 0.7 copy-start.17
  25.6 0.8 copy-start.5
  26.4 0.8 copy-start.7
  27.2 0.6 copy-start.12
  27.8 0.6 copy-start.14
  53.5 37.0 %copy-start.8 = (f32[1024,128]{1,0:T(8,128)S(1)}, f32[1024,128]{1,0:T(8,128)}, u32[]{:S(2)}) copy-start(f32[1024,128]{1,0:T(8,128)} %copy-done.7) | copy-start | bytes 1572868
  53.5 37.0 %copy-start.13 = (f32[3,64,128]{2,1,0:T(8,128)S(1)}, f32[3,64,128]{2,1,0:T(8,128)}, u32[]{:S(2)}) copy-start(f32[3,64,128]{2,1,0:T(8,128)} %copy-done.12) | copy-start | bytes 294916
  53.6 37.0 %copy-start.15 = (f32[192,128]{1,0:T(8,128)S(1)}, f32[192,128]{1,0:T(8,128)}, u32[]{:S(2)}) copy-start(f32[192,128]{1,0:T(8,128)} %copy-done.14) | copy-start | bytes 294916
  62.8 27.7 %copy-start.6 = (f32[1024,128]{1,0:T(8,128)S(1)}, f32[1024,128]{1,0:T(8,128)}, u32[]{:S(2)}) copy-start(f32[1024,128]{1,0:T(8,128)} %copy-done.5) | copy-start | bytes 1572868
  84.6 5.9 %copy-start.2 = (bf16[128,8,128]{2,1,0:T(8,128)(2,1)S(1)}, bf16[128,8,128]{2,1,0:T(8,128)(2,1)}, u32[]{:S(2)}) copy-start(bf16[128,8,128]{2,1,0:T(8,128)(2,1)} %all_to_all.15) | copy-start | bytes 786436
  86.5 11.4 %all-to-all-start.2 = ((f32[4,8,128]{2,1,0:T(8,128)}), f32[4,8,128]{2,1,0:T(8,128)S(1)}, u32[]{:S(2)}, u32[]{:S(2)}) async-start(f32[4,8,128]{2,1,0:T(8,128)} %norm.1), calls=%async_computation.2 | async-start | bytes 32768 | tf_op jit(solution)/shard_map/all_to_all | solution.py:659
  97.3 0.6 copy-start.16
  97.9 0.6 copy-start.18

commit v2 on v1

--- a/solution.py
+++ b/solution.py
@@ -15,8 +15,11 @@
 LANES = 128
 OWN = 8
 SUB = 8
-GROUP = 8
-STAGE = 99
+GROUP = 64
+TURNS = 4
+PREPARED = 10
+EDGE = 8
+SPAN = 24
 
 LEFT = LANES - 3 * REACH
 RIGHT = 0
@@ -60,17 +63,38 @@
     return lax.dot_general(a, b, (((1,), (1,)), ((), ())), preferred_element_type=F32)
 
 
-def turn_kernel(streams, cotangent, out):
-    for pair in range(2):
-        for k in range(SUB):
-            cols = pl.ds(k * LANES, LANES)
-            first = streams[2 * pair, :, cols]
-            second = streams[1, :, cols] if pair == 0 else cotangent[:, cols]
-            a = first.astype(F32).T.reshape(LANES // OWN, OWN, TOK)
-            b = second.astype(F32).T.reshape(LANES // OWN, OWN, TOK)
-            out[pl.ds(k * (LANES // OWN), LANES // OWN), pl.ds(pair * 16, 16), :] = (
-                jnp.concatenate([a, b], axis=1).astype(BF16)
+def turn_kernel(streams, cotangent, out, held, turned, arrive, leave):
+    wide = held.shape[3]
+    owners = wide // OWN
+    coming = []
+    for n in range(TURNS):
+        cols = pl.ds(n * wide, wide)
+        coming.append(
+            (
+                pltpu.make_async_copy(streams.at[:, :, cols], held.at[n, 0:3], arrive.at[n, 0]),
+                pltpu.make_async_copy(cotangent.at[:, cols], held.at[n, 3], arrive.at[n, 1]),
             )
+        )
+        for copy in coming[-1]:
+            copy.start()
+    going = []
+    for n in range(TURNS):
+        for copy in coming[n]:
+            copy.wait()
+        for pair in range(2):
+            for k in range(wide // LANES):
+                cols = pl.ds(k * LANES, LANES)
+                a, b = [
+                    held[n, 2 * pair + i, :, cols].astype(F32).T.reshape(LANES // OWN, OWN, TOK)
+                    for i in (0, 1)
+                ]
+                rows = pl.ds(n * owners + k * (LANES // OWN), LANES // OWN)
+                turned[rows, pl.ds(pair * 16, 16), :] = jnp.concatenate([a, b], axis=1).astype(BF16)
+        some = pl.ds(n * owners, owners)
+        going.append(pltpu.make_async_copy(turned.at[some], out.at[some], leave.at[n]))
+        going[-1].start()
+    for copy in going:
+        copy.wait()
 
 
 ROWS_OF = (0, 8, 16, 24)
@@ -140,8 +164,6 @@
         return 0
 
     lax.fori_loop(0, blocks // GROUP, filter_group, 0)
-    if STAGE < 2:
-        return
     for s in starts[:-1]:
         for near in (0, 1):
             b = jnp.minimum(s // TOK + near, blocks - 1)
@@ -162,8 +184,6 @@
         place = b * TOK + lane
         fixf[n * SUB : (n + 1) * SUB, :] = jnp.where(place >= starts[n], u[rows, :], 0.0)
         fixb[n * SUB : (n + 1) * SUB, :] = jnp.where(place < starts[n], dz[rows, :], 0.0)
-    if STAGE < 3:
-        return
 
     row = lax.broadcasted_iota(jnp.int32, (blocks, TOK), 0)
     col = lax.broadcasted_iota(jnp.int32, (blocks, TOK), 1)
@@ -189,11 +209,6 @@
     opening = jnp.concatenate(opening, axis=1)
     end_f = jnp.zeros((blocks, LANES), F32)
     end_b = jnp.zeros((blocks, LANES), F32)
-    if STAGE < 4:
-        zs[0:LANES, :] = head + tail + whole + lead_f[0].astype(F32) + lead_b[0].astype(F32)
-        zs[0:LANES, :] = ending[:, :LANES].astype(F32) + opening[:, :LANES].astype(F32)
-        zs[0:8, :] = taps
-        return
     for c in range(OWN):
         uc = (u[pl.ds(c, blocks, stride=OWN), :] * tail).astype(BF16)
         dc = (dz[pl.ds(c, blocks, stride=OWN), :] * head).astype(BF16)
@@ -201,9 +216,6 @@
         eb = dot_t(jnp.concatenate([dc, dc], axis=1), opening)
         end_f = jnp.where(mine == c, ef, end_f)
         end_b = jnp.where(mine == c, eb, end_b)
-    if STAGE < 5:
-        zs[0:LANES, :] = end_f + end_b
-        return
 
     keep_f = head[:, TOK - 1 : TOK] * whole
     keep_b = keep_f
@@ -220,10 +232,6 @@
     state_b = jnp.where(row < blocks - 1, pltpu.roll(end_b, blocks - 1, 0), 0.0)
     sf = halves(state_f)
     sb = halves(state_b)
-    if STAGE < 6:
-        zs[0:LANES, :] = sf[0].astype(F32) + sf[1].astype(F32)
-        zs[0:LANES, :] = sb[0].astype(F32) + sb[1].astype(F32)
-        return
 
     zero = jnp.zeros((blocks, LANES), BF16)
     every = jnp.concatenate([sf[0], sf[1], sb[0], sb[1]], axis=1)
@@ -257,8 +265,6 @@
         fixb[pl.ds(c, nseq, stride=OWN), :] = dot(few, nrek[0]) + dot(few, nrek[1])
         pick = jnp.where(lands & (pick_mine == c), 1.0, 0.0).astype(BF16)
         pay[pl.ds(c, blocks, stride=OWN), :] = dot(every, pick)
-    if STAGE < 7:
-        return
     for n in range(nseq):
         b = starts[n] // TOK
         rows = pl.ds(pl.multiple_of(b * SUB, SUB), SUB)
@@ -268,8 +274,6 @@
         if n > 0:
             fresh = (place >= starts[n - 1]) & (place < starts[n])
             ds[rows, :] = jnp.where(fresh, fixb[n * SUB : (n + 1) * SUB, :], ds[rows, :])
-    if STAGE < 8:
-        return
 
     def gradient_group(n, acc):
         acc = list(acc)
@@ -301,9 +305,6 @@
     grads = jnp.zeros((SUB, LANES), F32)
     for f in range(3 * TAPS):
         grads = jnp.where(lane == GRADS + f, jnp.sum(acc[f], axis=1, keepdims=True), grads)
-    if STAGE < 9:
-        zs[0:8, :] = grads
-        return
 
     def finish_group(n, _):
         b0 = n * GROUP
@@ -370,11 +371,36 @@
     return following - t
 
 
-def near(local, t0):
+def near(local, t0, count):
     found = jnp.bool_(False)
     for s in local:
-        found = found | ((s >= t0 - REACH) & (s < t0 + 8 + REACH + 1))
+        found = found | ((s >= t0 - REACH) & (s < t0 + count + REACH + 1))
     return found
+
+
+def added(terms):
+    while len(terms) > 1:
+        rest = terms[len(terms) // 2 * 2 :]
+        terms = [a + b for a, b in zip(terms[0::2], terms[1::2])] + rest
+    return terms[0]
+
+
+def scanned(prm, state, value, alive):
+    for m in range(MODES):
+        old = state[m]
+        if alive is not None:
+            old = jnp.where(alive, old, 0.0)
+        state[m] = tile(prm, m) * old + value
+    return added([tile(prm, MODES + m) * state[m] for m in range(MODES)])
+
+
+def carried(prm, state, alive):
+    for m in range(MODES):
+        old = state[m]
+        if alive is not None:
+            old = jnp.where(alive, old, 0.0)
+        state[m] = tile(prm, m) * old
+    return added(list(state))
 
 
 def eight_filtered(local, xs, ws, base, t0, masked):
@@ -397,7 +423,8 @@
 
 
 def prepare_kernel(
-    total, seq, streams, cotangent, weight, rate, gain, qs, ks, vs, cots, heads, ws, prm, xs
+    total, seq, streams, cotangent, weight, rate, gain,
+    heads, ws, prm, qs, zl, cots, ks, vs, dl, rl, xs, dzs,
 ):
     local = local_starts(total, seq)
     for k in range(SUB):
@@ -424,94 +451,95 @@
                         xs[i, rows, :] = part
                         if g == 0 and h == 0:
                             heads[i, rows, :] = part
-
-    def filtering(t0, masked):
+    for ref in (qs, ks, vs, zl, dl):
+        ref[0 : EDGE * SUB, :] = jnp.zeros((EDGE * SUB, LANES), F32)
+
+    def forward(t0, state, masked):
         done = eight_filtered(local, xs, ws, 0, t0, masked)
+        state = list(state)
         for r in range(8):
-            put(qs, t0 + r, done[0][r])
-            put(ks, t0 + r, done[1][r])
-            put(vs, t0 + r, done[2][r])
-
-    def step(n, _):
-        t0 = n * 8
-        close = near(local, t0)
-
-        @pl.when(close)
-        def _():
-            filtering(t0, True)
-
-        @pl.when(jnp.logical_not(close))
-        def _():
-            filtering(t0, False)
-
-        return 0
-
-    lax.fori_loop(1, TOK // 8, step, 0)
-
-
-def shard_kernel(
-    total, seq, fields, qs, ks, vs, cots, heads, ws, prm, out, grads_out, wgrad,
-    first, fs, q0, dzs, dfs, outs, sgs,
-):
+            t = t0 + r
+            q, k, v = done[0][r], done[1][r], done[2][r]
+            put(qs, t, q)
+            put(ks, t, k)
+            put(vs, t, v)
+            put(dzs, t, rounded(at(cots, t) * q))
+            alive = since(local, t) > 0 if masked else None
+            put(zl, t, scanned(prm, state, rounded(k * v), alive))
+        return tuple(state)
+
+    def backward(t0, state, masked):
+        state = list(state)
+        for r in range(7, -1, -1):
+            t = t0 + r
+            alive = until(local, t) > 1 if masked else None
+            put(dl, t, scanned(prm, state, at(dzs, t), alive))
+        return tuple(state)
+
+    def either(kernel, t0, state):
+        return lax.cond(
+            near(local, t0, 8),
+            lambda s: kernel(t0, s, True),
+            lambda s: kernel(t0, s, False),
+            state,
+        )
+
+    zeros = tuple(jnp.zeros((SUB, LANES), F32) for _ in range(MODES))
+    steps = (TOK - EDGE) // 8
+    lax.fori_loop(0, steps, lambda n, s: either(forward, EDGE + n * 8, s), zeros)
+    state = lax.fori_loop(0, steps, lambda n, s: either(backward, TOK - 8 - n * 8, s), zeros)
+    for m in range(MODES):
+        put(rl, m, state[m])
+
+
+def shard_kernel(total, seq, *refs):
+    far, refs = refs[: 1 + PREPARED], refs[1 + PREPARED :]
+    out, grads_out, wgrad, *refs = refs
+    held, refs = refs[: 1 + PREPARED], refs[1 + PREPARED :]
+    arrive, first, fs, q0, dz0, dfs, outs, sgs = refs
+    fields, heads, ws, prm, qs, zl, cots, ks, vs, dl, rl = held
+    coming = []
+    for n in range(1 + PREPARED):
+        coming.append(pltpu.make_async_copy(far[n], held[n], arrive.at[n]))
+        coming[-1].start()
     local = local_starts(total, seq)
+    coming[0].wait()
     for k in range(SUB):
         cols = pl.ds(k * LANES, LANES)
         turned = fields[pl.ds(k * LANES, LANES), :].astype(F32).T
         for g in range(LANES // 8):
             fs[pl.ds(g * 64 + k, 8, stride=SUB), :] = turned[g * 8 : g * 8 + 8]
+    for copy in coming[1:7]:
+        copy.wait()
     for i in range(3):
         first[i, 0 : REACH * SUB, :] = fs[(LEFT + i * REACH) * SUB : (LEFT + (i + 1) * REACH) * SUB, :]
-        first[i, REACH * SUB : (REACH + 8) * SUB, :] = heads[i]
+        first[i, REACH * SUB : (REACH + EDGE) * SUB, :] = heads[i]
         dfs[i, TOK * SUB : (TOK + REACH) * SUB, :] = fs[
             (RIGHT + i * REACH) * SUB : (RIGHT + (i + 1) * REACH) * SUB, :
         ]
-    done = eight_filtered(local, first, ws, REACH, 0, True)
-    for i in range(3):
-        for r in range(8):
-            put3(q0, i, r, done[i][r])
-
-    def forward(t0, state, masked, sources):
-        q_ref, k_ref, v_ref = sources
-        ages = [since(local, t0 + r) for r in range(8)] if masked else None
-        state = list(state)
-        for r in range(8):
-            t = t0 + r
-            q, c = at(q_ref, t), at(cots, t)
-            put(dzs, t, rounded(c * q))
-            u = rounded(at(k_ref, t) * at(v_ref, t))
-            z = jnp.zeros((SUB, LANES), F32)
-            for m in range(MODES):
-                old = state[m]
-                if masked:
-                    old = jnp.where(ages[r] > 0, old, 0.0)
-                state[m] = tile(prm, m) * old + u
-                z = z + tile(prm, MODES + m) * state[m]
-            z = rounded(z)
-            put(outs, t, q * z)
-            put3(dfs, 0, t, c * z)
-        return tuple(state)
-
-    def backward(t0, state, masked, sources):
-        _, k_ref, v_ref = sources
-        gaps = [until(local, t0 + r) for r in range(8)] if masked else None
-        state = list(state)
-        for r in range(7, -1, -1):
-            t = t0 + r
-            g = at(dzs, t)
-            d = jnp.zeros((SUB, LANES), F32)
-            for m in range(MODES):
-                old = state[m]
-                if masked:
-                    old = jnp.where(gaps[r] > 1, old, 0.0)
-                state[m] = tile(prm, m) * old + g
-                d = d + tile(prm, MODES + m) * state[m]
-            d = rounded(d)
-            put3(dfs, 1, t, d * at(v_ref, t))
-            put3(dfs, 2, t, d * at(k_ref, t))
+
+    def entering(g):
+        return [
+            tile(fs, STATE + g * MODES + m) + tile(fs, STATE + (g + 1) * MODES + m)
+            for m in range(MODES)
+        ]
+
+    def settle(t, q, z):
+        z = rounded(z)
+        put(outs, t, q * z)
+        put3(dfs, 0, t, at(cots, t) * z)
+
+    def settle_back(t, k, v, d):
+        d = rounded(d)
+        put3(dfs, 1, t, d * v)
+        put3(dfs, 2, t, d * k)
+
+    def adjoint(t0, count, masked):
+        gaps = [until(local, t0 + r) for r in range(count)] if masked else None
         for i in range(3):
             w = [tile(ws, i * 8 + j) for j in range(TAPS)]
-            y = [at3(dfs, i, t0 + n) for n in range(8 + REACH)]
-            for r in range(8):
+            y = [at3(dfs, i, t0 + n) for n in range(count + REACH)]
+            for r in range(count):
                 acc = w[0] * y[r]
                 for j in range(1, TAPS):
                     term = w[j] * y[r + j]
@@ -519,39 +547,60 @@
                         term = jnp.where(gaps[r] > j, term, 0.0)
                     acc = acc + term
                 put3(sgs, i, t0 + r, acc)
+
+    def forward(t0, state, masked):
+        state = list(state)
+        for r in range(SPAN):
+            t = t0 + r
+            alive = since(local, t) > 0 if masked else None
+            settle(t, at(qs, t), at(zl, t) + carried(prm, state, alive))
         return tuple(state)
 
-    def entering(g):
-        return tuple(
-            tile(fs, STATE + g * MODES + m) + tile(fs, STATE + (g + 1) * MODES + m)
-            for m in range(MODES)
-        )
-
-    edge = (q0.at[0], q0.at[1], q0.at[2])
-    whole = (qs, ks, vs)
-
-    def step_f(n, state):
-        t0 = n * 8
+    def backward(t0, state, masked):
+        state = list(state)
+        for r in range(SPAN - 1, -1, -1):
+            t = t0 + r
+            alive = until(local, t) > 1 if masked else None
+            settle_back(t, at(ks, t), at(vs, t), at(dl, t) + carried(prm, state, alive))
+        adjoint(t0, SPAN, masked)
+        return tuple(state)
+
+    def either(kernel, t0, state):
         return lax.cond(
-            near(local, t0),
-            lambda s: forward(t0, s, True, whole),
-            lambda s: forward(t0, s, False, whole),
+            near(local, t0, SPAN),
+            lambda s: kernel(t0, s, True),
+            lambda s: kernel(t0, s, False),
             state,
         )
 
-    def step_b(n, state):
-        t0 = TOK - 8 - n * 8
-        return lax.cond(
-            near(local, t0),
-            lambda s: backward(t0, s, True, whole),
-            lambda s: backward(t0, s, False, whole),
-            state,
-        )
-
-    state = forward(0, entering(0), True, edge)
-    lax.fori_loop(1, TOK // 8, step_f, state)
-    state = lax.fori_loop(0, TOK // 8 - 1, step_b, entering(2))
-    backward(0, state, True, edge)
+    def weighted(state):
+        return tuple(tile(prm, MODES + m) * state[m] for m in range(MODES))
+
+    done = eight_filtered(local, first, ws, REACH, 0, True)
+    state = entering(0)
+    for t in range(EDGE):
+        q, k, v = done[0][t], done[1][t], done[2][t]
+        put(dz0, t, rounded(at(cots, t) * q))
+        put3(q0, 0, t, k)
+        put3(q0, 1, t, v)
+        settle(t, q, scanned(prm, state, rounded(k * v), since(local, t) > 0))
+    steps = (TOK - EDGE) // SPAN
+    lax.fori_loop(0, steps, lambda n, s: either(forward, EDGE + n * SPAN, s), weighted(state))
+    for copy in coming[7:]:
+        copy.wait()
+    carry = lax.fori_loop(
+        0,
+        steps,
+        lambda n, s: either(backward, TOK - (n + 1) * SPAN, s),
+        weighted(entering(2)),
+    )
+    carry = list(carry)
+    state = [tile(rl, m) for m in range(MODES)]
+    for t in range(EDGE - 1, -1, -1):
+        alive = until(local, t) > 1
+        d = scanned(prm, state, at(dz0, t), alive) + carried(prm, carry, alive)
+        settle_back(t, at3(q0, 0, t), at3(q0, 1, t), d)
+    adjoint(0, EDGE, True)
 
     for k in range(SUB):
         cols = pl.ds(k * LANES, LANES)
@@ -588,6 +637,10 @@
             out[i, :, cols] = grads[i, :, cols] * factor
 
 
+def params(mebibytes):
+    return pltpu.CompilerParams(vmem_limit_bytes=mebibytes * 1024 * 1024)
+
+
 def vmem():
     return pl.BlockSpec(memory_space=pltpu.VMEM)
 
@@ -601,30 +654,37 @@
     shards = lax.axis_size("ctx")
     total = tok * shards
     rate_t, gain_t = rate.T, modal_gain.T
-    params = pltpu.CompilerParams(vmem_limit_bytes=48 * 1024 * 1024)
     turned = pl.pallas_call(
         turn_kernel,
         out_shape=jax.ShapeDtypeStruct((shards, 4 * OWN, tok), BF16),
-        in_specs=[vmem()] * 2,
-        out_specs=vmem(),
-        compiler_params=params,
+        in_specs=[pl.BlockSpec(memory_space=pl.ANY)] * 2,
+        out_specs=pl.BlockSpec(memory_space=pl.ANY),
+        scratch_shapes=[
+            pltpu.VMEM((TURNS, 4, tok, chans // TURNS), BF16),
+            pltpu.VMEM((shards, 4 * OWN, tok), BF16),
+            pltpu.SemaphoreType.DMA((TURNS, 2)),
+            pltpu.SemaphoreType.DMA((TURNS,)),
+        ],
+        compiler_params=params(60),
         name="turn",
     )(streams, cotangent)
     moved = lax.all_to_all(turned, "ctx", split_axis=0, concat_axis=0, tiled=True)
     plane = jax.ShapeDtypeStruct((tok * SUB, LANES), F32)
+    scratch = pltpu.VMEM((tok * SUB, LANES), F32)
     prepared = pl.pallas_call(
         functools.partial(prepare_kernel, total),
-        out_shape=[plane] * 4
-        + [
-            jax.ShapeDtypeStruct((3, 8 * SUB, LANES), F32),
+        out_shape=[
+            jax.ShapeDtypeStruct((3, EDGE * SUB, LANES), F32),
             jax.ShapeDtypeStruct((3 * 8 * SUB, LANES), F32),
             jax.ShapeDtypeStruct((2 * MODES * SUB, LANES), F32),
-        ],
+        ]
+        + [plane] * 6
+        + [jax.ShapeDtypeStruct((MODES * SUB, LANES), F32)],
         in_specs=[smem()] + [vmem()] * 5,
-        out_specs=[vmem()] * 7,
-        scratch_shapes=[pltpu.VMEM((3, tok * SUB, LANES), F32)],
-        compiler_params=params,
-        cost_estimate=pl.CostEstimate(flops=20_000_000, bytes_accessed=4_000_000, transcendentals=0),
+        out_specs=[vmem()] * PREPARED,
+        scratch_shapes=[pltpu.VMEM((3, tok * SUB, LANES), F32), scratch],
+        compiler_params=params(60),
+        cost_estimate=pl.CostEstimate(flops=40_000_000, bytes_accessed=6_000_000, transcendentals=0),
         name="prepare",
     )(seq_lengths, streams, cotangent, conv_weight, rate_t, gain_t)
     moved, *prepared = lax.optimization_barrier((moved, *prepared))
@@ -642,7 +702,7 @@
         + [plane] * 8
         + [pltpu.VMEM((8 * SUB, LANES), F32)] * 2
         + [pltpu.VMEM((LANES, LANES), F32)],
-        compiler_params=params,
+        compiler_params=params(22),
         name="owner",
     )(seq_lengths, moved, conv_weight, rate_t, gain_t)
     fields = lax.all_to_all(
@@ -654,10 +714,10 @@
         out_shape=jax.ShapeDtypeStruct((planes, SUB, LANES), F32),
         in_specs=[vmem()],
         out_specs=vmem(),
+        compiler_params=params(60),
         name="norm",
     )(fields)
     squares = lax.all_to_all(partial, "ch", split_axis=0, concat_axis=0, tiled=True)
-    scratch = pltpu.VMEM((tok * SUB, LANES), F32)
     output, stream_grads, weight_grad = pl.pallas_call(
         functools.partial(shard_kernel, total),
         out_shape=[
@@ -665,18 +725,20 @@
             jax.ShapeDtypeStruct((3, tok, chans), BF16),
             jax.ShapeDtypeStruct((3, TAPS, chans), F32),
         ],
-        in_specs=[smem()] + [vmem()] * 8,
+        in_specs=[smem()] + [pl.BlockSpec(memory_space=pl.ANY)] * (1 + PREPARED),
         out_specs=[vmem()] * 3,
-        scratch_shapes=[
-            pltpu.VMEM((3, (REACH + 8) * SUB, LANES), F32),
+        scratch_shapes=[pltpu.VMEM(x.shape, x.dtype) for x in (fields, *prepared)]
+        + [
+            pltpu.SemaphoreType.DMA((1 + PREPARED,)),
+            pltpu.VMEM((3, (REACH + EDGE) * SUB, LANES), F32),
             pltpu.VMEM((LANES * SUB, LANES), F32),
-            pltpu.VMEM((3, 8 * SUB, LANES), F32),
-            scratch,
+            pltpu.VMEM((2, EDGE * SUB, LANES), F32),
+            pltpu.VMEM((EDGE * SUB, LANES), F32),
             pltpu.VMEM((3, (tok + REACH) * SUB, LANES), F32),
             scratch,
             pltpu.VMEM((3, tok * SUB, LANES), F32),
         ],
-        compiler_params=params,
+        compiler_params=params(60),
         cost_estimate=pl.CostEstimate(flops=40_000_000, bytes_accessed=6_000_000, transcendentals=0),
         name="shard",
     )(seq_lengths, fields, *prepared)
@@ -685,6 +747,7 @@
         out_shape=jax.ShapeDtypeStruct(weight_grad.shape, F32),
         in_specs=[vmem()] * 2,
         out_specs=vmem(),
+        compiler_params=params(60),
         name="clip",
     )(weight_grad, squares)
     return output, stream_grads, clipped

time: 101 us -> 96.1 us (0.951)
  local copies, waits for them, and re-layouts: 6.82 us -> 1.26 us
  Pallas kernels: 23.1 us -> 26.4 us
  waiting for transfers between devices: 25.1 us -> 23.3 us
    unnamed x38 -> x10, local copies, waits for them, and re-layouts: 6.82 us -> 1.26 us
    pallas_call x1, Pallas kernels: 2.28 us -> 7.62 us  [body(): pl.pallas_call(functools.partial(prepare_kernel, total), out_shape=[jax.S...]
    pallas_call x1, Pallas kernels: 9.29 us -> 6.82 us  [body(): pl.pallas_call(functools.partial(owner_kernel, total), out_shape=jax.Shap...]
    all_to_all x1, waiting for transfers between devices: 25.1 us -> 23.2 us  [body(): lax.all_to_all(turned, 'ctx', split_axis=0, concat_axis=0, tiled=True)]
  transfers between devices with their start and end apart: 2 -> 2, of which waited for: 1 -> 1; matrix products, arithmetic and copies ran while one was open for 0% -> 0% of each run, Pallas kernels for 9% -> 15%
where the time goes in v2:
time: 96.1 us; the launch traced here: 95.7 us
  Pallas kernels  26.4 us (27%)
  waiting for transfers between devices  23.3 us (24%)
  starting transfers between devices  22.4 us (23%)
  blocking collectives  21.6 us (22%)
  local copies, waits for them, and re-layouts  1.26 us (1%)
    all_to_all x1, waiting for transfers between devices, body(): lax.all_to_all(turned, 'ctx', split_axis=0, concat_axis=0, tiled=True)  23.2 us
    all_to_all x1, blocking collectives, body(): lax.all_to_all(payload.reshape(shards, OWN, LANES), 'ctx', split_axis=0,...  21.6 us
    all_to_all x1, starting transfers between devices, body(): lax.all_to_all(turned, 'ctx', split_axis=0, concat_axis=0, tiled=True)  18.4 us
    pallas_call x1, Pallas kernels, body(): pl.pallas_call(functools.partial(prepare_kernel, total), out_shape=[jax.S...  7.62 us
    pallas_call x1, Pallas kernels, body(): pl.pallas_call(functools.partial(owner_kernel, total), out_shape=jax.Shap...  6.82 us
    pallas_call x1, Pallas kernels, body(): pl.pallas_call(functools.partial(shard_kernel, total), out_shape=[jax.Sha...  6.28 us
    all_to_all x1, starting transfers between devices, body(): lax.all_to_all(partial, 'ch', split_axis=0, concat_axis=0, tiled=True)  4.01 us
    pallas_call x1, Pallas kernels, body(): pl.pallas_call(turn_kernel, out_shape=jax.ShapeDtypeStruct((shards, 4 * O...  2.3 us
  transfers between devices with their start and end apart: 2, of which 1 were waited for; matrix products, arithmetic and copies ran while one was open for 0% of the time, Pallas kernels for 15%

profile of v2, /device:TPU:1, one launch (start us, length us, event | category | flops | bytes accessed | tf_op | source)
XLA Modules:
  0.0 95.7 jit_solution(3238673882615463920)
XLA Ops:
  0.6 2.3 %turn.1 = bf16[128,32,128]{2,1,0:T(8,128)(2,1)} custom-call(bf16[3,128,1024]{2,1,0:T(8,128)(2,1)} %streams.3, bf16[128,1024]{1,0:T(8,128)(2,1)} %cotangent.3), custom_call_target="tpu_custom_call" | custom-call | tf_op jit(solution)/shard_map/turn/pallas_call | solution.py:657
  2.9 18.4 %all-to-all-start = ((bf16[128,32,128]{2,1,0:T(8,128)(2,1)}), bf16[128,32,128]{2,1,0:T(8,128)(2,1)S(1)}, u32[]{:S(2)}, u32[]{:S(2)}) async-start(bf16[128,32,128]{2,1,0:T(8,128)(2,1)} %turn.1), calls=%async_computation | async-start | bytes 2097152 | tf_op jit(solution)/shard_map/all_to_all | solution.py:671
  21.4 0.0 copy-start
  21.4 0.0 copy-start.1
  21.4 0.0 copy-start.2
  21.4 7.6 %prepare.1 = (f32[3,64,128]{2,1,0:T(8,128)}, f32[192,128]{1,0:T(8,128)}, f32[256,128]{1,0:T(8,128)}, f32[1024,128]{1,0:T(8,128)}, f32[1024,128]{1,0:T(8,128)}, /...) custom-call(s32[8]{0:T(128)} %seq.5, ...), custom_call_target="tpu_custom_call" | custom-call | flops 40000000 | bytes 6000000 | tf_op jit(solution)/shard_map/prepare/pallas_call | solution.py:674
  29.0 23.2 %all-to-all-done.moved = bf16[128,32,128]{2,1,0:T(8,128)(2,1)S(1)} async-done(((bf16[128,32,128]{2,1,0:T(8,128)(2,1)}), bf16[128,32,128]{2,1,0:T(8,128)(2,1)S(1)}, u32[]{:S(2)}, u32[]{:S(2)}) %all-to-all-start) | async-done | bytes 1048608 | tf_op jit(solution)/shard_map/all_to_all | solution.py:671
  52.3 0.0 copy-start.3
  52.3 0.0 copy-done
  52.3 0.0 copy-done.1
  52.3 0.0 copy-done.2
  52.3 0.6 copy-done.3
  52.9 6.8 %owner.1 = bf16[1024,128]{1,0:T(8,128)(2,1)S(1)} custom-call(s32[8]{0:T(128)S(1)} %copy-done.3, bf16[128,32,128]{2,1,0:T(8,128)(2,1)S(1)} %all-to-all-done.moved, f32[3,7,1024]{2,1,0:T(8,128)S(1)} %copy-done, f32[16,1024]{1,0:T(8,128)S(1)} %bitcast.6, f32[16,1024]{1,0:T(8,128)S(1)} %bitcast.8), custom_call_target="tpu_custom_call" | custom-call | tf_op jit(solution)/shard_map/owner/pallas_call | solution.py:693
  59.8 21.6 %all_to_all.15 = bf16[128,8,128]{2,1,0:T(8,128)(2,1)} all-to-all(bf16[128,8,128]{2,1,0:T(8,128)(2,1)S(1)} %bitcast.4), channel_id=1, replica_groups=mesh['ctx'=128,'ch'=4] {'ctx'}, dimensions={0} | all-to-all | bytes 524288 | tf_op jit(solution)/shard_map/all_to_all | solution.py:708
  81.4 1.8 %norm.1 = f32[4,8,128]{2,1,0:T(8,128)} custom-call(bf16[1024,128]{1,0:T(8,128)(2,1)} %bitcast.9), custom_call_target="tpu_custom_call" | custom-call | tf_op jit(solution)/shard_map/norm/pallas_call | solution.py:712
  83.2 4.0 %all-to-all-start.2 = ((f32[4,8,128]{2,1,0:T(8,128)}), f32[4,8,128]{2,1,0:T(8,128)S(1)}, u32[]{:S(2)}, u32[]{:S(2)}) async-start(f32[4,8,128]{2,1,0:T(8,128)} %norm.1), calls=%async_computation.2 | async-start | bytes 32768 | tf_op jit(solution)/shard_map/all_to_all | solution.py:720
  87.2 6.3 %shard.1 = (bf16[128,1024]{1,0:T(8,128)(2,1)}, bf16[3,128,1024]{2,1,0:T(8,128)(2,1)}, f32[3,7,1024]{2,1,0:T(8,128)}) custom-call(s32[8]{0:T(128)} %seq.5, bf16[1024,128]{1,0:T(8,128)(2,1)} %bitcast.10, f32[3,64,128]{2,1,0:T(8,128)} %get-tuple-element.38.refs_1_, f32[192,128]{1,0:T(8,128)} %get-tuple-element.39.refs_2_, ...), custom_call_target="tpu_custom_call" | custom-call | flops 40000000 | bytes 6000000 | tf_op jit(solution)/shard_map/shard/pallas_call | solution.py:721
  93.5 0.0 all-to-all-done.2.squares
  93.5 0.0 copy-start.4
  93.5 0.6 copy-done.4
  94.1 1.6 %clip.1 = f32[3,7,1024]{2,1,0:T(8,128)} custom-call(f32[3,7,1024]{2,1,0:T(8,128)} %get-tuple-element.50.grads, f32[4,8,128]{2,1,0:T(8,128)} %copy-done.4), custom_call_target="tpu_custom_call" | custom-call | tf_op jit(solution)/shard_map/clip/pallas_call | solution.py:745
Async XLA Ops:
  2.9 49.3 %all-to-all-start = ((bf16[128,32,128]{2,1,0:T(8,128)(2,1)}), bf16[128,32,128]{2,1,0:T(8,128)(2,1)S(1)}, u32[]{:S(2)}, u32[]{:S(2)}) async-start(bf16[128,32,128]{2,1,0:T(8,128)(2,1)} %turn.1), calls=%async_computation | async-start | bytes 2097152 | tf_op jit(solution)/shard_map/all_to_all | solution.py:671
  21.4 30.9 %copy-start = (f32[3,7,1024]{2,1,0:T(8,128)S(1)}, f32[3,7,1024]{2,1,0:T(8,128)}, u32[]{:S(2)}) copy-start(f32[3,7,1024]{2,1,0:T(8,128)} %weight.3) | copy-start | bytes 258052
  21.4 30.9 %copy-start.1 = (f32[1024,16]{0,1:T(8,128)S(1)}, f32[1024,16]{0,1:T(8,128)}, u32[]{:S(2)}) copy-start(f32[1024,16]{0,1:T(8,128)} %param.9) | copy-start | bytes 196612
  21.4 30.9 %copy-start.2 = (f32[1024,16]{0,1:T(8,128)S(1)}, f32[1024,16]{0,1:T(8,128)}, u32[]{:S(2)}) copy-start(f32[1024,16]{0,1:T(8,128)} %param.10) | copy-start | bytes 196612
  52.3 0.7 copy-start.3
  83.2 10.3 %all-to-all-start.2 = ((f32[4,8,128]{2,1,0:T(8,128)}), f32[4,8,128]{2,1,0:T(8,128)S(1)}, u32[]{:S(2)}, u32[]{:S(2)}) async-start(f32[4,8,128]{2,1,0:T(8,128)} %norm.1), calls=%async_computation.2 | async-start | bytes 32768 | tf_op jit(solution)/shard_map/all_to_all | solution.py:720
  93.5 0.6 copy-start.4

commit v3 on v2

--- a/solution.py
+++ b/solution.py
@@ -19,7 +19,7 @@
 TURNS = 4
 PREPARED = 10
 EDGE = 8
-SPAN = 24
+SPAN = 40
 
 LEFT = LANES - 3 * REACH
 RIGHT = 0
@@ -496,21 +496,34 @@
     far, refs = refs[: 1 + PREPARED], refs[1 + PREPARED :]
     out, grads_out, wgrad, *refs = refs
     held, refs = refs[: 1 + PREPARED], refs[1 + PREPARED :]
-    arrive, first, fs, q0, dz0, dfs, outs, sgs = refs
+    arrive, leave, out_held, grads_held, wgrad_held, first, fs, q0, dz0, dfs, outs, sgs = refs
     fields, heads, ws, prm, qs, zl, cots, ks, vs, dl, rl = held
-    coming = []
-    for n in range(1 + PREPARED):
-        coming.append(pltpu.make_async_copy(far[n], held[n], arrive.at[n]))
-        coming[-1].start()
+    coming = [None] + [
+        pltpu.make_async_copy(far[n], held[n], arrive.at[n]) for n in range(1, 1 + PREPARED)
+    ]
+    halves_in = [
+        pltpu.make_async_copy(
+            far[0].at[pl.ds(h * 512, 512)], held[0].at[pl.ds(h * 512, 512)], arrive.at[h * (1 + PREPARED)]
+        )
+        for h in (0, 1)
+    ]
+    for copy in halves_in:
+        copy.start()
     local = local_starts(total, seq)
-    coming[0].wait()
     for k in range(SUB):
-        cols = pl.ds(k * LANES, LANES)
+        if k == 0:
+            halves_in[0].wait()
+        if k == SUB // 2:
+            halves_in[1].wait()
+            for copy in coming[1:7]:
+                copy.start()
         turned = fields[pl.ds(k * LANES, LANES), :].astype(F32).T
         for g in range(LANES // 8):
             fs[pl.ds(g * 64 + k, 8, stride=SUB), :] = turned[g * 8 : g * 8 + 8]
     for copy in coming[1:7]:
         copy.wait()
+    for copy in coming[7:]:
+        copy.start()
     for i in range(3):
         first[i, 0 : REACH * SUB, :] = fs[(LEFT + i * REACH) * SUB : (LEFT + (i + 1) * REACH) * SUB, :]
         first[i, REACH * SUB : (REACH + EDGE) * SUB, :] = heads[i]
@@ -586,6 +599,28 @@
         settle(t, q, scanned(prm, state, rounded(k * v), since(local, t) > 0))
     steps = (TOK - EDGE) // SPAN
     lax.fori_loop(0, steps, lambda n, s: either(forward, EDGE + n * SPAN, s), weighted(state))
+
+    def finished(rows_of, target):
+        for k in range(SUB):
+            for g in range(TOK // 16):
+                both = jnp.concatenate(
+                    [rows_of(pl.ds((g * 16 + h * 8) * SUB + k, 8, stride=SUB)) for h in (0, 1)],
+                    axis=0,
+                )
+                target[pl.ds(g * 16, 16), pl.ds(k * LANES, LANES)] = both.astype(BF16)
+
+    for k in range(SUB):
+        for i in range(3):
+            wgrad_held[i, :, pl.ds(k * LANES, LANES)] = fs[
+                pl.ds((GRADS + i * TAPS) * SUB + k, TAPS, stride=SUB), :
+            ]
+    finished(lambda rows: outs[rows, :], out_held)
+    going = [
+        pltpu.make_async_copy(wgrad_held, wgrad, leave.at[3]),
+        pltpu.make_async_copy(out_held, out, leave.at[4]),
+    ]
+    for copy in going:
+        copy.start()
     for copy in coming[7:]:
         copy.wait()
     carry = lax.fori_loop(
@@ -602,21 +637,12 @@
         settle_back(t, at3(q0, 0, t), at3(q0, 1, t), d)
     adjoint(0, EDGE, True)
 
-    for k in range(SUB):
-        cols = pl.ds(k * LANES, LANES)
-        for i in range(3):
-            wgrad[i, :, cols] = fs[pl.ds((GRADS + i * TAPS) * SUB + k, TAPS, stride=SUB), :]
-        for g in range(TOK // 16):
-            for i in range(4):
-                parts = []
-                for h in range(2):
-                    rows = pl.ds((g * 16 + h * 8) * SUB + k, 8, stride=SUB)
-                    parts.append(sgs[i, rows, :] if i < 3 else outs[rows, :])
-                both = jnp.concatenate(parts, axis=0).astype(BF16)
-                if i < 3:
-                    grads_out[i, pl.ds(g * 16, 16), cols] = both
-                else:
-                    out[pl.ds(g * 16, 16), cols] = both
+    for i in range(3):
+        finished(lambda rows: sgs[i, rows, :], grads_held.at[i])
+        going.append(pltpu.make_async_copy(grads_held.at[i], grads_out.at[i], leave.at[i]))
+        going[-1].start()
+    for copy in going:
+        copy.wait()
 
 
 def norm_kernel(fields, out):
@@ -726,10 +752,14 @@
             jax.ShapeDtypeStruct((3, TAPS, chans), F32),
         ],
         in_specs=[smem()] + [pl.BlockSpec(memory_space=pl.ANY)] * (1 + PREPARED),
-        out_specs=[vmem()] * 3,
+        out_specs=[pl.BlockSpec(memory_space=pl.ANY)] * 3,
         scratch_shapes=[pltpu.VMEM(x.shape, x.dtype) for x in (fields, *prepared)]
         + [
-            pltpu.SemaphoreType.DMA((1 + PREPARED,)),
+            pltpu.SemaphoreType.DMA((2 + PREPARED,)),
+            pltpu.SemaphoreType.DMA((5,)),
+            pltpu.VMEM((tok, chans), BF16),
+            pltpu.VMEM((3, tok, chans), BF16),
+            pltpu.VMEM((3, TAPS, chans), F32),
             pltpu.VMEM((3, (REACH + EDGE) * SUB, LANES), F32),
             pltpu.VMEM((LANES * SUB, LANES), F32),
             pltpu.VMEM((2, EDGE * SUB, LANES), F32),

time: 96.1 us -> 97.2 us (1.011)
  Pallas kernels: 26.4 us -> 27.4 us
    pallas_call x1, Pallas kernels: 6.28 us -> 7.29 us  [body(): pl.pallas_call(functools.partial(shard_kernel, total), out_shape=[jax.Sha...]
where the time goes in v3:
time: 97.2 us; the launch traced here: 96.7 us
  Pallas kernels  27.4 us (28%)
  waiting for transfers between devices  23.3 us (24%)
  starting transfers between devices  22.4 us (23%)
  blocking collectives  21.6 us (22%)
  local copies, waits for them, and re-layouts  1.26 us (1%)
    all_to_all x1, waiting for transfers between devices, body(): lax.all_to_all(turned, 'ctx', split_axis=0, concat_axis=0, tiled=True)  23.2 us
    all_to_all x1, blocking collectives, body(): lax.all_to_all(payload.reshape(shards, OWN, LANES), 'ctx', split_axis=0,...  21.6 us
    all_to_all x1, starting transfers between devices, body(): lax.all_to_all(turned, 'ctx', split_axis=0, concat_axis=0, tiled=True)  18.4 us
    pallas_call x1, Pallas kernels, body(): pl.pallas_call(functools.partial(prepare_kernel, total), out_shape=[jax.S...  7.62 us
    pallas_call x1, Pallas kernels, body(): pl.pallas_call(functools.partial(shard_kernel, total), out_shape=[jax.Sha...  7.29 us
    pallas_call x1, Pallas kernels, body(): pl.pallas_call(functools.partial(owner_kernel, total), out_shape=jax.Shap...  6.81 us
    all_to_all x1, starting transfers between devices, body(): lax.all_to_all(partial, 'ch', split_axis=0, concat_axis=0, tiled=True)  4.01 us
    pallas_call x1, Pallas kernels, body(): pl.pallas_call(turn_kernel, out_shape=jax.ShapeDtypeStruct((shards, 4 * O...  2.3 us
  transfers between devices with their start and end apart: 2, of which 1 were waited for; matrix products, arithmetic and copies ran while one was open for 0% of the time, Pallas kernels for 15%

profile of v3, /device:TPU:1, one launch (start us, length us, event | category | flops | bytes accessed | tf_op | source)
XLA Modules:
  0.0 96.7 jit_solution(1955332419918408368)
XLA Ops:
  0.6 2.3 %turn.1 = bf16[128,32,128]{2,1,0:T(8,128)(2,1)} custom-call(bf16[3,128,1024]{2,1,0:T(8,128)(2,1)} %streams.3, bf16[128,1024]{1,0:T(8,128)(2,1)} %cotangent.3), custom_call_target="tpu_custom_call" | custom-call | tf_op jit(solution)/shard_map/turn/pallas_call | solution.py:683
  2.9 18.4 %all-to-all-start = ((bf16[128,32,128]{2,1,0:T(8,128)(2,1)}), bf16[128,32,128]{2,1,0:T(8,128)(2,1)S(1)}, u32[]{:S(2)}, u32[]{:S(2)}) async-start(bf16[128,32,128]{2,1,0:T(8,128)(2,1)} %turn.1), calls=%async_computation | async-start | bytes 2097152 | tf_op jit(solution)/shard_map/all_to_all | solution.py:697
  21.4 0.0 copy-start
  21.4 0.0 copy-start.1
  21.4 0.0 copy-start.2
  21.4 7.6 %prepare.1 = (f32[3,64,128]{2,1,0:T(8,128)}, f32[192,128]{1,0:T(8,128)}, f32[256,128]{1,0:T(8,128)}, f32[1024,128]{1,0:T(8,128)}, f32[1024,128]{1,0:T(8,128)}, /...) custom-call(s32[8]{0:T(128)} %seq.5, ...), custom_call_target="tpu_custom_call" | custom-call | flops 40000000 | bytes 6000000 | tf_op jit(solution)/shard_map/prepare/pallas_call | solution.py:700
  29.0 23.2 %all-to-all-done.moved = bf16[128,32,128]{2,1,0:T(8,128)(2,1)S(1)} async-done(((bf16[128,32,128]{2,1,0:T(8,128)(2,1)}), bf16[128,32,128]{2,1,0:T(8,128)(2,1)S(1)}, u32[]{:S(2)}, u32[]{:S(2)}) %all-to-all-start) | async-done | bytes 1048608 | tf_op jit(solution)/shard_map/all_to_all | solution.py:697
  52.3 0.0 copy-start.3
  52.3 0.0 copy-done
  52.3 0.0 copy-done.1
  52.3 0.0 copy-done.2
  52.3 0.6 copy-done.3
  52.9 6.8 %owner.1 = bf16[1024,128]{1,0:T(8,128)(2,1)S(1)} custom-call(s32[8]{0:T(128)S(1)} %copy-done.3, bf16[128,32,128]{2,1,0:T(8,128)(2,1)S(1)} %all-to-all-done.moved, f32[3,7,1024]{2,1,0:T(8,128)S(1)} %copy-done, f32[16,1024]{1,0:T(8,128)S(1)} %bitcast.6, f32[16,1024]{1,0:T(8,128)S(1)} %bitcast.8), custom_call_target="tpu_custom_call" | custom-call | tf_op jit(solution)/shard_map/owner/pallas_call | solution.py:719
  59.8 21.6 %all_to_all.15 = bf16[128,8,128]{2,1,0:T(8,128)(2,1)} all-to-all(bf16[128,8,128]{2,1,0:T(8,128)(2,1)S(1)} %bitcast.4), channel_id=1, replica_groups=mesh['ctx'=128,'ch'=4] {'ctx'}, dimensions={0} | all-to-all | bytes 524288 | tf_op jit(solution)/shard_map/all_to_all | solution.py:734
  81.4 1.8 %norm.1 = f32[4,8,128]{2,1,0:T(8,128)} custom-call(bf16[1024,128]{1,0:T(8,128)(2,1)} %bitcast.9), custom_call_target="tpu_custom_call" | custom-call | tf_op jit(solution)/shard_map/norm/pallas_call | solution.py:738
  83.2 4.0 %all-to-all-start.2 = ((f32[4,8,128]{2,1,0:T(8,128)}), f32[4,8,128]{2,1,0:T(8,128)S(1)}, u32[]{:S(2)}, u32[]{:S(2)}) async-start(f32[4,8,128]{2,1,0:T(8,128)} %norm.1), calls=%async_computation.2 | async-start | bytes 32768 | tf_op jit(solution)/shard_map/all_to_all | solution.py:746
  87.2 7.3 %shard.1 = (bf16[128,1024]{1,0:T(8,128)(2,1)}, bf16[3,128,1024]{2,1,0:T(8,128)(2,1)}, f32[3,7,1024]{2,1,0:T(8,128)}) custom-call(s32[8]{0:T(128)} %seq.5, bf16[1024,128]{1,0:T(8,128)(2,1)} %bitcast.10, f32[3,64,128]{2,1,0:T(8,128)} %get-tuple-element.38.refs_1_, f32[192,128]{1,0:T(8,128)} %get-tuple-element.39.refs_2_, ...), custom_call_target="tpu_custom_call" | custom-call | flops 40000000 | bytes 6000000 | tf_op jit(solution)/shard_map/shard/pallas_call | solution.py:747
  94.5 0.0 all-to-all-done.2.squares
  94.5 0.0 copy-start.4
  94.5 0.6 copy-done.4
  95.1 1.6 %clip.1 = f32[3,7,1024]{2,1,0:T(8,128)} custom-call(f32[3,7,1024]{2,1,0:T(8,128)} %get-tuple-element.50.grads, f32[4,8,128]{2,1,0:T(8,128)} %copy-done.4), custom_call_target="tpu_custom_call" | custom-call | tf_op jit(solution)/shard_map/clip/pallas_call | solution.py:775
Async XLA Ops:
  2.9 49.3 %all-to-all-start = ((bf16[128,32,128]{2,1,0:T(8,128)(2,1)}), bf16[128,32,128]{2,1,0:T(8,128)(2,1)S(1)}, u32[]{:S(2)}, u32[]{:S(2)}) async-start(bf16[128,32,128]{2,1,0:T(8,128)(2,1)} %turn.1), calls=%async_computation | async-start | bytes 2097152 | tf_op jit(solution)/shard_map/all_to_all | solution.py:697
  21.4 30.9 %copy-start = (f32[3,7,1024]{2,1,0:T(8,128)S(1)}, f32[3,7,1024]{2,1,0:T(8,128)}, u32[]{:S(2)}) copy-start(f32[3,7,1024]{2,1,0:T(8,128)} %weight.3) | copy-start | bytes 258052
  21.4 30.9 %copy-start.1 = (f32[1024,16]{0,1:T(8,128)S(1)}, f32[1024,16]{0,1:T(8,128)}, u32[]{:S(2)}) copy-start(f32[1024,16]{0,1:T(8,128)} %param.9) | copy-start | bytes 196612
  21.4 30.9 %copy-start.2 = (f32[1024,16]{0,1:T(8,128)S(1)}, f32[1024,16]{0,1:T(8,128)}, u32[]{:S(2)}) copy-start(f32[1024,16]{0,1:T(8,128)} %param.10) | copy-start | bytes 196612
  52.3 0.7 copy-start.3
  83.2 11.3 %all-to-all-start.2 = ((f32[4,8,128]{2,1,0:T(8,128)}), f32[4,8,128]{2,1,0:T(8,128)S(1)}, u32[]{:S(2)}, u32[]{:S(2)}) async-start(f32[4,8,128]{2,1,0:T(8,128)} %norm.1), calls=%async_computation.2 | async-start | bytes 32768 | tf_op jit(solution)/shard_map/all_to_all | solution.py:746
  94.5 0.6 copy-start.4

commit v4 on v3

--- a/solution.py
+++ b/solution.py
@@ -498,32 +498,19 @@
     held, refs = refs[: 1 + PREPARED], refs[1 + PREPARED :]
     arrive, leave, out_held, grads_held, wgrad_held, first, fs, q0, dz0, dfs, outs, sgs = refs
     fields, heads, ws, prm, qs, zl, cots, ks, vs, dl, rl = held
-    coming = [None] + [
-        pltpu.make_async_copy(far[n], held[n], arrive.at[n]) for n in range(1, 1 + PREPARED)
-    ]
-    halves_in = [
-        pltpu.make_async_copy(
-            far[0].at[pl.ds(h * 512, 512)], held[0].at[pl.ds(h * 512, 512)], arrive.at[h * (1 + PREPARED)]
-        )
-        for h in (0, 1)
-    ]
-    for copy in halves_in:
-        copy.start()
+    coming = []
+    for n in range(1 + PREPARED):
+        coming.append(pltpu.make_async_copy(far[n], held[n], arrive.at[n]))
+        coming[-1].start()
     local = local_starts(total, seq)
+    coming[0].wait()
     for k in range(SUB):
-        if k == 0:
-            halves_in[0].wait()
-        if k == SUB // 2:
-            halves_in[1].wait()
-            for copy in coming[1:7]:
-                copy.start()
+        cols = pl.ds(k * LANES, LANES)
         turned = fields[pl.ds(k * LANES, LANES), :].astype(F32).T
         for g in range(LANES // 8):
             fs[pl.ds(g * 64 + k, 8, stride=SUB), :] = turned[g * 8 : g * 8 + 8]
     for copy in coming[1:7]:
         copy.wait()
-    for copy in coming[7:]:
-        copy.start()
     for i in range(3):
         first[i, 0 : REACH * SUB, :] = fs[(LEFT + i * REACH) * SUB : (LEFT + (i + 1) * REACH) * SUB, :]
         first[i, REACH * SUB : (REACH + EDGE) * SUB, :] = heads[i]
@@ -755,7 +742,7 @@
         out_specs=[pl.BlockSpec(memory_space=pl.ANY)] * 3,
         scratch_shapes=[pltpu.VMEM(x.shape, x.dtype) for x in (fields, *prepared)]
         + [
-            pltpu.SemaphoreType.DMA((2 + PREPARED,)),
+            pltpu.SemaphoreType.DMA((1 + PREPARED,)),
             pltpu.SemaphoreType.DMA((5,)),
             pltpu.VMEM((tok, chans), BF16),
             pltpu.VMEM((3, tok, chans), BF16),

time: 97.2 us -> 95.9 us (0.987)
  Pallas kernels: 27.4 us -> 26.1 us
    pallas_call x1, Pallas kernels: 7.29 us -> 5.96 us  [body(): pl.pallas_call(functools.partial(shard_kernel, total), out_shape=[jax.Sha...]
  transfers between devices with their start and end apart: 2 -> 2, of which waited for: 1 -> 1; matrix products, arithmetic and copies ran while one was open for 0% -> 0% of each run, Pallas kernels for 15% -> 14%
where the time goes in v4:
time: 95.9 us; the launch traced here: 95.4 us
  Pallas kernels  26.1 us (27%)
  waiting for transfers between devices  23.3 us (24%)
  starting transfers between devices  22.4 us (23%)
  blocking collectives  21.6 us (23%)
  local copies, waits for them, and re-layouts  1.26 us (1%)
    all_to_all x1, waiting for transfers between devices, body(): lax.all_to_all(turned, 'ctx', split_axis=0, concat_axis=0, tiled=True)  23.2 us
    all_to_all x1, blocking collectives, body(): lax.all_to_all(payload.reshape(shards, OWN, LANES), 'ctx', split_axis=0,...  21.6 us
    all_to_all x1, starting transfers between devices, body(): lax.all_to_all(turned, 'ctx', split_axis=0, concat_axis=0, tiled=True)  18.4 us
    pallas_call x1, Pallas kernels, body(): pl.pallas_call(functools.partial(prepare_kernel, total), out_shape=[jax.S...  7.62 us
    pallas_call x1, Pallas kernels, body(): pl.pallas_call(functools.partial(owner_kernel, total), out_shape=jax.Shap...  6.81 us
    pallas_call x1, Pallas kernels, body(): pl.pallas_call(functools.partial(shard_kernel, total), out_shape=[jax.Sha...  5.96 us
    all_to_all x1, starting transfers between devices, body(): lax.all_to_all(partial, 'ch', split_axis=0, concat_axis=0, tiled=True)  4.01 us
    pallas_call x1, Pallas kernels, body(): pl.pallas_call(turn_kernel, out_shape=jax.ShapeDtypeStruct((shards, 4 * O...  2.3 us
  transfers between devices with their start and end apart: 2, of which 1 were waited for; matrix products, arithmetic and copies ran while one was open for 0% of the time, Pallas kernels for 14%

profile of v4, /device:TPU:1, one launch (start us, length us, event | category | flops | bytes accessed | tf_op | source)
XLA Modules:
  0.0 95.4 jit_solution(6679815543504152799)
XLA Ops:
  0.6 2.3 %turn.1 = bf16[128,32,128]{2,1,0:T(8,128)(2,1)} custom-call(bf16[3,128,1024]{2,1,0:T(8,128)(2,1)} %streams.3, bf16[128,1024]{1,0:T(8,128)(2,1)} %cotangent.3), custom_call_target="tpu_custom_call" | custom-call | tf_op jit(solution)/shard_map/turn/pallas_call | solution.py:670
  2.9 18.4 %all-to-all-start = ((bf16[128,32,128]{2,1,0:T(8,128)(2,1)}), bf16[128,32,128]{2,1,0:T(8,128)(2,1)S(1)}, u32[]{:S(2)}, u32[]{:S(2)}) async-start(bf16[128,32,128]{2,1,0:T(8,128)(2,1)} %turn.1), calls=%async_computation | async-start | bytes 2097152 | tf_op jit(solution)/shard_map/all_to_all | solution.py:684
  21.4 0.0 copy-start
  21.4 0.0 copy-start.1
  21.4 0.0 copy-start.2
  21.4 7.6 %prepare.1 = (f32[3,64,128]{2,1,0:T(8,128)}, f32[192,128]{1,0:T(8,128)}, f32[256,128]{1,0:T(8,128)}, f32[1024,128]{1,0:T(8,128)}, f32[1024,128]{1,0:T(8,128)}, /...) custom-call(s32[8]{0:T(128)} %seq.5, ...), custom_call_target="tpu_custom_call" | custom-call | flops 40000000 | bytes 6000000 | tf_op jit(solution)/shard_map/prepare/pallas_call | solution.py:687
  29.0 23.2 %all-to-all-done.moved = bf16[128,32,128]{2,1,0:T(8,128)(2,1)S(1)} async-done(((bf16[128,32,128]{2,1,0:T(8,128)(2,1)}), bf16[128,32,128]{2,1,0:T(8,128)(2,1)S(1)}, u32[]{:S(2)}, u32[]{:S(2)}) %all-to-all-start) | async-done | bytes 1048608 | tf_op jit(solution)/shard_map/all_to_all | solution.py:684
  52.3 0.0 copy-start.3
  52.3 0.0 copy-done
  52.3 0.0 copy-done.1
  52.3 0.0 copy-done.2
  52.3 0.6 copy-done.3
  52.9 6.8 %owner.1 = bf16[1024,128]{1,0:T(8,128)(2,1)S(1)} custom-call(s32[8]{0:T(128)S(1)} %copy-done.3, bf16[128,32,128]{2,1,0:T(8,128)(2,1)S(1)} %all-to-all-done.moved, f32[3,7,1024]{2,1,0:T(8,128)S(1)} %copy-done, f32[16,1024]{1,0:T(8,128)S(1)} %bitcast.6, f32[16,1024]{1,0:T(8,128)S(1)} %bitcast.8), custom_call_target="tpu_custom_call" | custom-call | tf_op jit(solution)/shard_map/owner/pallas_call | solution.py:706
  59.8 21.6 %all_to_all.15 = bf16[128,8,128]{2,1,0:T(8,128)(2,1)} all-to-all(bf16[128,8,128]{2,1,0:T(8,128)(2,1)S(1)} %bitcast.4), channel_id=1, replica_groups=mesh['ctx'=128,'ch'=4] {'ctx'}, dimensions={0} | all-to-all | bytes 524288 | tf_op jit(solution)/shard_map/all_to_all | solution.py:721
  81.4 1.8 %norm.1 = f32[4,8,128]{2,1,0:T(8,128)} custom-call(bf16[1024,128]{1,0:T(8,128)(2,1)} %bitcast.9), custom_call_target="tpu_custom_call" | custom-call | tf_op jit(solution)/shard_map/norm/pallas_call | solution.py:725
  83.2 4.0 %all-to-all-start.2 = ((f32[4,8,128]{2,1,0:T(8,128)}), f32[4,8,128]{2,1,0:T(8,128)S(1)}, u32[]{:S(2)}, u32[]{:S(2)}) async-start(f32[4,8,128]{2,1,0:T(8,128)} %norm.1), calls=%async_computation.2 | async-start | bytes 32768 | tf_op jit(solution)/shard_map/all_to_all | solution.py:733
  87.2 6.0 %shard.1 = (bf16[128,1024]{1,0:T(8,128)(2,1)}, bf16[3,128,1024]{2,1,0:T(8,128)(2,1)}, f32[3,7,1024]{2,1,0:T(8,128)}) custom-call(s32[8]{0:T(128)} %seq.5, bf16[1024,128]{1,0:T(8,128)(2,1)} %bitcast.10, f32[3,64,128]{2,1,0:T(8,128)} %get-tuple-element.38.refs_1_, f32[192,128]{1,0:T(8,128)} %get-tuple-element.39.refs_2_, ...), custom_call_target="tpu_custom_call" | custom-call | flops 40000000 | bytes 6000000 | tf_op jit(solution)/shard_map/shard/pallas_call | solution.py:734
  93.2 0.0 all-to-all-done.2.squares
  93.2 0.0 copy-start.4
  93.2 0.6 copy-done.4
  93.8 1.6 %clip.1 = f32[3,7,1024]{2,1,0:T(8,128)} custom-call(f32[3,7,1024]{2,1,0:T(8,128)} %get-tuple-element.50.grads, f32[4,8,128]{2,1,0:T(8,128)} %copy-done.4), custom_call_target="tpu_custom_call" | custom-call | tf_op jit(solution)/shard_map/clip/pallas_call | solution.py:762
Async XLA Ops:
  2.9 49.3 %all-to-all-start = ((bf16[128,32,128]{2,1,0:T(8,128)(2,1)}), bf16[128,32,128]{2,1,0:T(8,128)(2,1)S(1)}, u32[]{:S(2)}, u32[]{:S(2)}) async-start(bf16[128,32,128]{2,1,0:T(8,128)(2,1)} %turn.1), calls=%async_computation | async-start | bytes 2097152 | tf_op jit(solution)/shard_map/all_to_all | solution.py:684
  21.4 30.9 %copy-start = (f32[3,7,1024]{2,1,0:T(8,128)S(1)}, f32[3,7,1024]{2,1,0:T(8,128)}, u32[]{:S(2)}) copy-start(f32[3,7,1024]{2,1,0:T(8,128)} %weight.3) | copy-start | bytes 258052
  21.4 30.9 %copy-start.1 = (f32[1024,16]{0,1:T(8,128)S(1)}, f32[1024,16]{0,1:T(8,128)}, u32[]{:S(2)}) copy-start(f32[1024,16]{0,1:T(8,128)} %param.9) | copy-start | bytes 196612
  21.4 30.9 %copy-start.2 = (f32[1024,16]{0,1:T(8,128)S(1)}, f32[1024,16]{0,1:T(8,128)}, u32[]{:S(2)}) copy-start(f32[1024,16]{0,1:T(8,128)} %param.10) | copy-start | bytes 196612
  52.3 0.7 copy-start.3
  83.2 10.0 %all-to-all-start.2 = ((f32[4,8,128]{2,1,0:T(8,128)}), f32[4,8,128]{2,1,0:T(8,128)S(1)}, u32[]{:S(2)}, u32[]{:S(2)}) async-start(f32[4,8,128]{2,1,0:T(8,128)} %norm.1), calls=%async_computation.2 | async-start | bytes 32768 | tf_op jit(solution)/shard_map/all_to_all | solution.py:733
  93.2 0.6 copy-start.4
